TPU v7x, 256 devices: a whole 4x4x8 slice. The times are simulated.
256 devices in a mesh: gx: 16 (over z, y_lo), yz: 16 (over y_hi, x, core).
Axes of the slice: x: 4, y: 4 (y_hi: 2, y_lo: 2; y = y_hi * 2 + y_lo), z: 8, core: 2. Of those that a mesh axis runs over, the one named last changes fastest.
Arguments:
- positions: float32 [16, 16, 3, 80], P('gx', 'yz'), may hold values from -1 to 138, as said below
- velocities: float32 [16, 16, 3, 80], P('gx', 'yz'), may hold values from -4 to 4
- forces: float32 [16, 16, 3, 80], P('gx', 'yz'), may hold values from -4 to 4
- species: int32 [16, 16, 80], P('gx', 'yz'), may hold values from 0 to 4
- neighbours: int32 [16, 16, 96, 80], P('gx', 'yz'), may hold values from 0 to 319, as said below
- slot_mask: int32 [16, 16, 96, 80], P('gx', 'yz'), may hold values from 0 to 1
- send_x: int32 [16, 16, 2, 40], P('gx', 'yz'), may hold values from 0 to 79, as said below
- send_y: int32 [16, 16, 2, 80], P('gx', 'yz'), may hold values from 0 to 159, as said below
- move_send: int32 [16, 16, 2, 5], P('gx', 'yz'), may hold values from 0 to 80, as said below
- move_recv: int32 [16, 16, 2, 5], P('gx', 'yz'), may hold values from 0 to 80, as said below
- w_bessel: float32 [8, 32], replicated, may hold values from -2 to 2
- emb_center: float32 [32, 5], replicated, may hold values from -4 to 4
- emb_neigh: float32 [32, 5], replicated, may hold values from -4 to 4
- w_env: float32 [32, 32], replicated, may hold values from -1 to 1
- w_latent: float32 [128, 32], replicated, may hold values from -0.5 to 0.5
- w_out: float32 [32], replicated, may hold values from -1 to 1
Outputs:
- new_velocity: float32 [16, 16, 3, 80], P('gx', 'yz')
- new_travel: float32 [16, 16, 3, 80], P('gx', 'yz')
Inputs may be any that keep to these rules, and one draw needn't show every extreme that they name: `positions`: positions lie near a cubic lattice of spacing 2.15 whose sites fill each brick (4 by 4 by 5 sites); z is periodic over the brick. `neighbours`: rows of the brick's table: 80 owned rows, 40 ghosts from the lower gx neighbour, 40 from the upper, 80 from the lower yz neighbour, 80 from the upper, each ghost block in its sender's list order. Valid slots name distinct atoms other than the slot's own. `send_x`: rows 0 and 1 are disjoint. `send_y`: rows 0 and 1 are disjoint. `move_send`: 80 marks an empty slot; filled slots come first and name distinct rows; some brick fills all 5 slots of both rows. `move_recv`: 80 exactly where the sender's matching entry is 80; other entries are distinct rows that are vacant or leave.
All inputs are finite; a program needn't handle non-finite values.
Results may differ from a plain program's by a relative error of at most 0.0003.
Values sent between devices are 32-bit elements; how exact they have to be, the bound alone decides.
A program may use at most 64 MiB of HBM per device.

v0:
```python
import jax
import jax.numpy as jnp
from jax import lax
from jax.experimental import pallas as pl
from jax.experimental.pallas import tpu as pltpu
from jax.sharding import PartitionSpec as P

PX = 4
PY = 4
PZ = 5
STEPS = 1
SPACING = 2.15
CUTOFF = 6.0
TIME_STEP = 0.05
ENV_SCALE = 0.125
MASSES = (1.008, 12.011, 14.007, 15.999, 32.06)
HIGHEST = lax.Precision.HIGHEST
MESH = pl.DeviceIdType.MESH
F32 = jnp.float32
BF16 = jnp.bfloat16
I32 = jnp.int32

LANES = 128
GROUP = 16
PI = 3.141592653589793
R3 = 3.0**0.5
R5 = 5.0**0.5
R15 = 15.0**0.5

HALO = [(dx, dy) for dy in (-1, 0, 1) for dx in (-1, 0, 1)]
NEAR = [pos for pos in HALO if pos != (0, 0)]
TARGETS = [(dx, dy) for dy in (-1, 0, 1) for dx in (-2, -1, 0, 1, 2)]
FAR = [pos for pos in TARGETS if pos != (0, 0)]


def halo_slot(dx, dy):
    return (dy + 1) * 3 + dx + 1


def target_slot(dx, dy):
    return (dy + 1) * 5 + dx + 2


def nt_dot(a, b, precision=None):
    return lax.dot_general(
        a, b, (((1,), (1,)), ((), ())), precision=precision, preferred_element_type=F32
    )


def nn_dot(a, b, precision=None):
    return jnp.dot(a, b, precision=precision, preferred_element_type=F32)


def halves(x):
    high = x.astype(BF16)
    low = (x - high.astype(F32)).astype(BF16)
    return high, low


def left_parts(w):
    high, low = halves(w)
    return jnp.concatenate([high, high, low], axis=1)


def right_parts(x):
    high, low = halves(x)
    return jnp.concatenate([high, low, high], axis=0)


def pick(rows, index):
    return jnp.take_along_axis(rows, index, axis=1, mode="promise_in_bounds")


def sigmoid(x):
    return 1.0 / (1.0 + jnp.exp(-x))


def lanes_total(x):
    for shift in (64, 32, 16):
        x = x + pltpu.roll(x, shift, 1)
    return x


def kernel_body(
    period,
    atoms,
    slots,
    pos_ref,
    vel_ref,
    frc_ref,
    spc_ref,
    nbr_ref,
    msk_ref,
    sx_ref,
    sy_ref,
    ms_ref,
    mr_ref,
    wb_ref,
    ec_ref,
    en_ref,
    we_ref,
    wl_ref,
    wo_ref,
    nv_ref,
    ntr_ref,
    halo,
    load,
    ret_out,
    ret_in,
    nb_pad,
    rows_code,
    table,
    sc,
    zf,
    zy,
    zd,
    pt,
    cterm,
    mats,
    w1s,
    wcol,
    pre_s,
    sig_s,
    ef_s,
    dlp_s,
    hid_s,
    gs,
    dfs,
    g3,
    halo_send,
    halo_recv,
    load_send,
    load_recv,
    ret_send,
    ret_recv,
):
    gx = lax.axis_index("gx")
    yz = lax.axis_index("yz")
    n_gx = lax.axis_size("gx")
    n_yz = lax.axis_size("yz")
    blocks = atoms // GROUP
    per_block = slots // 8
    n_rows = blocks * per_block
    chunks = (n_rows + 7) // 8

    def device(dx, dy):
        return (lax.rem(gx + dx + n_gx, n_gx), lax.rem(yz + dy + n_yz, n_yz))

    barrier = pltpu.get_barrier_semaphore()
    for dx, dy in FAR:
        pl.semaphore_signal(barrier, inc=1, device_id=device(dx, dy), device_id_type=MESH)

    lane1 = lax.broadcasted_iota(I32, (1, LANES), 1)
    lane8 = lax.broadcasted_iota(I32, (8, LANES), 1)
    sub8 = lax.broadcasted_iota(I32, (8, LANES), 0)

    own = halo_slot(0, 0)
    kinds = spc_ref[0].astype(F32)
    minv = jnp.zeros_like(kinds)
    for kind, mass in enumerate(MASSES):
        minv = jnp.where(kinds == float(kind), 1.0 / jnp.float32(mass), minv)
    start = pos_ref[0, 0]
    velocity = vel_ref[0, 0] + 0.5 * TIME_STEP * frc_ref[0, 0] * minv
    coords = start + TIME_STEP * velocity
    travel = (coords - start) / (STEPS * TIME_STEP)
    halo[own] = jnp.zeros((8, LANES), F32)
    load[1] = jnp.zeros((8, LANES), F32)
    halo[own, 0:3, 0:atoms] = coords
    halo[own, 3:4, 0:atoms] = kinds
    code = lane1
    place = lane1
    source = lane1
    for side in (0, 1):
        for k in range(ms_ref.shape[3]):
            seat = atoms + 5 * (1 - side) + k
            code = jnp.where(lane1 == mr_ref[0, 0, side, k], LANES - 1, code)
    for side in (0, 1):
        for k in range(ms_ref.shape[3]):
            seat = atoms + 5 * (1 - side) + k
            gone = ms_ref[0, 0, side, k]
            code = jnp.where(lane1 == gone, (2 * side - 1) * LANES + seat, code)
            place = jnp.where(lane1 == seat, gone, place)
            source = jnp.where(lane1 == gone, LANES - 1, source)
    for side in (0, 1):
        for k in range(ms_ref.shape[3]):
            source = jnp.where(lane1 == mr_ref[0, 0, side, k], atoms + 5 * side + k, source)
    code = jnp.where(lane1 < atoms, code + LANES, 0)
    halo[own, 4:5, :] = code.astype(F32)
    halo[own, 6:8, 0:atoms] = sy_ref[0, 0].astype(F32)
    load[1, 0:3, 0:atoms] = velocity
    load[1, 3:6, 0:atoms] = travel
    load[1, 6:7, 0:atoms] = minv
    width_x = sx_ref.shape[3]
    g3[0] = jnp.zeros((64, LANES), F32)
    g3[0, 0:2, 0:width_x] = sx_ref[0, 0].astype(F32)
    lists = g3[0, 0:8, :]
    halo[own, 5:6, :] = lists[1:2] + pltpu.roll(lists, width_x, 1)[0:1]
    load[1] = pick(load[1], jnp.broadcast_to(place, (8, LANES)))

    pl.semaphore_wait(barrier, len(FAR))
    sends = []
    for dx, dy in NEAR:
        there = halo_slot(-dx, -dy)
        copy = pltpu.make_async_remote_copy(
            src_ref=halo.at[own],
            dst_ref=halo.at[there],
            send_sem=halo_send.at[there],
            recv_sem=halo_recv.at[there],
            device_id=device(dx, dy),
            device_id_type=MESH,
        )
        copy.start()
        sends.append(copy)
    for dx in (-1, 1):
        there = 1 - dx
        copy = pltpu.make_async_remote_copy(
            src_ref=load.at[1],
            dst_ref=load.at[there],
            send_sem=load_send.at[there],
            recv_sem=load_recv.at[there],
            device_id=device(dx, 0),
            device_id_type=MESH,
        )
        copy.start()
        sends.append(copy)

    nb_pad[...] = jnp.zeros((slots, LANES), F32)
    nb_pad[:, 0:atoms] = nbr_ref[0, 0].astype(F32) + 512.0 * msk_ref[0, 0].astype(F32)
    rows_code[...] = jnp.zeros((chunks * 8, LANES), F32)
    in_group = lane8 // GROUP == sub8
    for block in range(blocks):
        spread = (lane8 & (GROUP - 1)) + block * GROUP
        for jb in range(per_block):
            moved = pick(nb_pad[jb * 8 : jb * 8 + 8, :], spread)
            row = jnp.sum(jnp.where(in_group, moved, 0.0), axis=0, keepdims=True)
            r = block * per_block + jb
            rows_code[r : r + 1, :] = row

    ch = we_ref.shape[0]
    eye = (
        lax.broadcasted_iota(I32, (ch, ch), 0) == lax.broadcasted_iota(I32, (ch, ch), 1)
    ).astype(F32)
    for part in range(3):
        mixed = ENV_SCALE * nn_dot(we_ref[...], wl_ref[(part + 1) * ch : (part + 2) * ch, :], HIGHEST)
        mats[2 + part] = left_parts(nt_dot(eye, mixed, HIGHEST))
        mats[5 + part] = left_parts(mixed)
    mats[0] = left_parts(nt_dot(eye, wl_ref[0:ch, :], HIGHEST))
    mats[1] = left_parts(wl_ref[0:ch, :])
    n_basis = wb_ref.shape[0]
    n_kinds = en_ref.shape[1]
    w1f = jnp.concatenate(
        [
            nt_dot(eye, wb_ref[...], HIGHEST),
            en_ref[...],
            jnp.zeros((ch, 16 - n_basis - n_kinds), F32),
        ],
        axis=1,
    )
    w1s[...] = left_parts(w1f)
    w_basis = left_parts(wb_ref[...])
    wcol[...] = jnp.broadcast_to(
        jnp.sum(jnp.where(eye > 0, wo_ref[...], 0.0), axis=1, keepdims=True), (ch, LANES)
    )

    for copy in sends:
        copy.wait()

    def shifted(dx, dy):
        step = float(LANES * ((dy + 1) * 5 + dx + 1))
        return halo[halo_slot(dx, dy)] + jnp.where(sub8 == 4, step, 0.0)

    def row_index(rows, which):
        return jnp.broadcast_to(rows[which : which + 1, :], (8, LANES)).astype(I32)

    def x_ghosts(dy):
        low, high = shifted(-1, dy), shifted(1, dy)
        return jnp.where(
            lane8 < width_x,
            pick(low, row_index(low, 5)),
            pick(high, row_index(high, 5)),
        )

    def y_ghosts(dy):
        base = shifted(0, dy)
        index = row_index(base, 7 if dy < 0 else 6)
        outer = index >= atoms
        return jnp.where(
            outer,
            pick(x_ghosts(dy), jnp.where(outer, index - atoms, 0)),
            pick(base, jnp.where(outer, 0, index)),
        )

    table[0] = shifted(0, 0)
    table[1] = x_ghosts(0)
    table[2] = y_ghosts(-1)
    table[3] = y_ghosts(1)

    def whole(k, c):
        return jnp.broadcast_to(table[k, c : c + 1, :], (8, LANES))

    def forward_chunk(i, carry):
        word = rows_code[pl.ds(pl.multiple_of(i * 8, 8), 8), :]
        live = word >= 512.0
        n = jnp.where(live, word - 512.0, word).astype(I32)
        k = jnp.where(n >= atoms, 1, 0) + jnp.where(n >= 2 * atoms, 1, 0) + jnp.where(n >= 3 * atoms, 1, 0)
        n = n - atoms * k
        near = []
        for c in range(5):
            v = pick(whole(0, c), n)
            for part in (1, 2, 3):
                v = jnp.where(k == part, pick(whole(part, c), n), v)
            near.append(v)
        row = i * 8 + sub8
        block = jnp.zeros((8, LANES), I32)
        for b in range(1, blocks):
            block = block + jnp.where(row >= b * per_block, 1, 0)
        centre = block * GROUP + (lane8 & (GROUP - 1))
        off = []
        for c in range(3):
            d = near[c] - pick(whole(0, c), centre)
            d = d - period[c] * jnp.floor(d / period[c] + 0.5)
            off.append(jnp.where(live, d, SPACING if c == 0 else 0.0))
        radius = jnp.sqrt(off[0] * off[0] + off[1] * off[1] + off[2] * off[2])
        rinv = 1.0 / radius
        ux, uy, uz = (o * rinv for o in off)
        q = radius / CUTOFF
        valid = jnp.logical_and(live, q < 1.0)
        q2 = q * q
        q5 = q2 * q2 * q
        q6 = q5 * q
        env = jnp.where(valid, 1.0 + q6 * (-28.0 + q * (48.0 - 21.0 * q)), 0.0)
        denv = jnp.where(valid, (168.0 / CUTOFF) * q5 * (-1.0 + q * (2.0 - q)), 0.0)
        u = PI * jnp.minimum(q, 1.0) - 0.5 * PI
        w = u * u
        sin1 = 1.0 + w * (-1 / 2 + w * (1 / 24 + w * (-1 / 720 + w * (1 / 40320 + w * (-1 / 3628800 + w * (1 / 479001600))))))
        cos1 = -u * (1.0 + w * (-1 / 6 + w * (1 / 120 + w * (-1 / 5040 + w * (1 / 362880 + w * (-1 / 39916800 + w * (1 / 6227020800)))))))
        sc[0, i] = ux
        sc[1, i] = uy
        sc[2, i] = uz
        sc[3, i] = rinv
        sc[4, i] = denv
        zbase = i * 128
        scale = (2.0 / CUTOFF) ** 0.5 * rinv
        s_prev, s_now = jnp.zeros_like(sin1), sin1
        c_prev, c_now = jnp.ones_like(cos1), cos1
        for order in range(1, n_basis + 1):
            bes = scale * s_now
            zf[pl.ds(zbase + order - 1, 8, stride=16), :] = bes
            sc[4 + order, i] = scale * (order * PI / CUTOFF) * c_now - bes * rinv
            s_prev, s_now = s_now, 2.0 * cos1 * s_now - s_prev
            c_prev, c_now = c_now, 2.0 * cos1 * c_now - c_prev
        for kind in range(n_kinds):
            zf[pl.ds(zbase + n_basis + kind, 8, stride=16), :] = jnp.where(near[3] == float(kind), 1.0, 0.0)
        for extra in range(n_basis + n_kinds, 16):
            zf[pl.ds(zbase + extra, 8, stride=16), :] = jnp.zeros((8, LANES), F32)
        ys = (
            R3 * ux,
            R3 * uy,
            R3 * uz,
            R15 * ux * uy,
            R15 * uy * uz,
            0.5 * R5 * (3.0 * uz * uz - 1.0),
            R15 * ux * uz,
            0.5 * R15 * (ux * ux - uy * uy),
        )
        for m, y in enumerate(ys):
            zy[pl.ds(zbase + m, 8, stride=16), :] = y
        zy[pl.ds(zbase + 8, 8, stride=16), :] = env
        dest = near[4].astype(I32)
        tbase = i * 64
        pt[pl.ds(tbase + 6, 8, stride=8), :] = (dest >> 7).astype(F32)
        pt[pl.ds(tbase + 7, 8, stride=8), :] = (dest & (LANES - 1)).astype(F32)
        return carry

    lax.fori_loop(0, chunks, forward_chunk, 0)

    for block in range(blocks):
        spread = (lane8 & (GROUP - 1)) + block * GROUP
        kind_row = jnp.broadcast_to(pick(whole(0, 3), spread)[0:1], (ch, LANES))
        term = jnp.zeros((ch, LANES), F32)
        for kind in range(n_kinds):
            term = jnp.where(
                kind_row == float(kind),
                jnp.broadcast_to(ec_ref[:, kind : kind + 1], (ch, LANES)),
                term,
            )
        cterm[block] = term

    degrees = (0, 1, 1, 1, 2, 2, 2, 2, 2)

    def y_rows(row):
        return [zy[pl.ds(row * 16 + m, 1), :] for m in range(9)]

    def by_degree(first, parts):
        out = []
        for degree, (a, b) in enumerate(((0, 1), (1, 4), (4, 9))):
            joined = jnp.concatenate(parts[a:b], axis=1)
            got = nn_dot(mats[first + degree], right_parts(joined))
            out += [got[:, t * LANES : (t + 1) * LANES] for t in range(b - a)]
        return out

    def block_body(block, carry):
        base = block * per_block
        feats = jnp.concatenate(
            [zf[pl.ds(pl.multiple_of((base + jb) * 16, 16), 16), :] for jb in range(per_block)], axis=1
        )
        pre = nn_dot(w1s[...], right_parts(feats))
        centre_term = cterm[block]
        acc = None
        for jb in range(per_block):
            p = pre[:, jb * LANES : (jb + 1) * LANES] + centre_term
            *ys, env = y_rows(base + jb)
            sig = sigmoid(p)
            ef = p * sig * env
            pre_s[jb] = p
            sig_s[jb] = sig
            ef_s[jb] = ef
            new = [ef] + [ef * y for y in ys]
            acc = new if acc is None else [a + b for a, b in zip(acc, new)]
        sums = [lanes_total(a) for a in acc]
        grow = by_degree(2, sums)
        for m in range(9):
            gs[m] = grow[m]
        mixed = nn_dot(mats[0], right_parts(jnp.concatenate([ef_s[jb] for jb in range(per_block)], axis=1)))
        acc = None
        w_out = wcol[...]
        for jb in range(per_block):
            *ys, env = y_rows(base + jb)
            lp = mixed[:, jb * LANES : (jb + 1) * LANES] + gs[0]
            for m in range(8):
                lp = lp + gs[m + 1] * ys[m]
            sig = sigmoid(lp)
            lat = lp * sig
            hid_s[jb] = w_out * (ef_s[jb] + lat)
            dlp = (w_out * env) * (sig + lat * (1.0 - sig))
            dlp_s[jb] = dlp
            new = [dlp] + [dlp * y for y in ys]
            acc = new if acc is None else [a + b for a, b in zip(acc, new)]
        sums = [lanes_total(a) for a in acc]
        grow = by_degree(5, sums)
        for m in range(9):
            dfs[m] = grow[m]
        mixed = nn_dot(mats[1], right_parts(jnp.concatenate([dlp_s[jb] for jb in range(per_block)], axis=1)))
        dps = []
        for jb in range(per_block):
            *ys, env = y_rows(base + jb)
            de = mixed[:, jb * LANES : (jb + 1) * LANES] + w_out * env + dfs[0]
            for m in range(8):
                de = de + dfs[m + 1] * ys[m]
            sig = sig_s[jb]
            s1 = pre_s[jb] * sig
            dps.append(de * env * (sig + s1 * (1.0 - sig)))
            zbase = (base + jb) * 24
            zd[pl.ds(zbase + 16, 1), :] = jnp.sum(hid_s[jb] + de * s1, axis=0, keepdims=True)
            ef, dlp = ef_s[jb], dlp_s[jb]
            for m in range(8):
                zd[pl.ds(zbase + 8 + m, 1), :] = jnp.sum(
                    gs[m + 1] * dlp + dfs[m + 1] * ef, axis=0, keepdims=True
                )
        dbes = nn_dot(w_basis, right_parts(jnp.concatenate(dps, axis=1)))
        for jb in range(per_block):
            zd[pl.ds(pl.multiple_of((base + jb) * 24, 8), 8), :] = dbes[:, jb * LANES : (jb + 1) * LANES]
        return carry

    lax.fori_loop(0, blocks, block_body, 0)
    for row in range(n_rows, chunks * 8):
        zd[row * 24 : row * 24 + 24, :] = jnp.zeros((24, LANES), F32)

    def put_parts(store, values):
        for c in range(3):
            high = values[c].astype(BF16).astype(F32)
            store(c, high)
            store(c + 3, values[c] - high)

    def backward_chunk(i, carry):
        zbase = i * 192

        def d(which):
            return zd[pl.ds(zbase + which, 8, stride=24), :]

        ux, uy, uz, rinv, denv = (sc[t, i] for t in range(5))
        dr = d(16) * denv
        for order in range(n_basis):
            dr = dr + d(order) * sc[5 + order, i]
        d1, d2, d3, d4, d5, d6, d7, d8 = (d(8 + m) for m in range(8))
        dux = R3 * d1 + R15 * (uy * d4 + uz * d7 + ux * d8)
        duy = R3 * d2 + R15 * (ux * d4 + uz * d5 - uy * d8)
        duz = R3 * d3 + R15 * (uy * d5 + ux * d7) + (3.0 * R5) * uz * d6
        radial = dr - rinv * (dux * ux + duy * uy + duz * uz)
        forces = [-(radial * u + rinv * du) for u, du in ((ux, dux), (uy, duy), (uz, duz))]
        at = pl.ds(pl.multiple_of(i * 8, 8), 8)
        for c in range(3):
            g3[c, at, :] = forces[c]

        def store(which, value):
            pt[pl.ds(i * 64 + which, 8, stride=8), :] = value

        put_parts(store, forces)
        return carry

    lax.fori_loop(0, chunks, backward_chunk, 0)

    extra = chunks * 8
    pt[extra * 8 :, :] = jnp.zeros((8 * 8, LANES), F32)
    for block in range(blocks):
        at = (extra + block) * 8
        sums = [
            -jnp.sum(g3[c, block * per_block : (block + 1) * per_block, :], axis=0, keepdims=True)
            for c in range(3)
        ]

        def store(which, value):
            pt[at + which : at + which + 1, :] = value

        put_parts(store, sums)
        spread = (lane8 & (GROUP - 1)) + block * GROUP
        dest = pick(whole(0, 4), spread)[0:1].astype(I32)
        pt[at + 6 : at + 7, :] = (dest >> 7).astype(F32)
        pt[at + 7 : at + 8, :] = (dest & (LANES - 1)).astype(F32)

    n_targets = len(TARGETS)
    tall = 96
    sub_tall = lax.broadcasted_iota(I32, (tall, LANES), 0).astype(F32)

    def scatter_body(i, acc):
        lefts, rights = [], []
        for t in range(8):
            v = pt[pl.ds(pl.multiple_of((i * 8 + t) * 8, 8), 8), :]
            where_to, lo = v[6:7], v[7:8]
            lefts.append(
                jnp.concatenate([jnp.where(where_to == float(b), v, 0.0) for b in range(n_targets)], axis=0)
            )
            rights.append(jnp.where(lo == sub_tall, 1.0, 0.0))
        left = jnp.concatenate(lefts, axis=1).astype(BF16)
        right = jnp.concatenate(rights, axis=1).astype(BF16)
        return acc + nt_dot(left, right)

    spread_out = lax.fori_loop(
        0, chunks + 1, scatter_body, jnp.zeros((n_targets * 8, tall), F32)
    )
    for t in range(n_targets):
        ret_out[t] = jnp.zeros((8, LANES), F32)
        ret_out[t, :, 0:tall] = spread_out[t * 8 : t * 8 + 8, :]

    sends = []
    for dx, dy in FAR:
        there = target_slot(-dx, -dy)
        copy = pltpu.make_async_remote_copy(
            src_ref=ret_out.at[target_slot(dx, dy)],
            dst_ref=ret_in.at[there],
            send_sem=ret_send.at[there],
            recv_sem=ret_recv.at[there],
            device_id=device(dx, dy),
            device_id_type=MESH,
        )
        copy.start()
        sends.append(copy)

    settle = jnp.broadcast_to(source, (8, LANES))
    mine, low, high = load[1], load[0], load[2]
    held = jnp.where(lane8 < atoms, mine, jnp.where(lane8 < atoms + 5, low, high))
    held = jnp.where(lane8 < LANES - 1, held, 0.0)
    held = pick(held, settle)
    total = ret_out[target_slot(0, 0)]
    for copy, (dx, dy) in zip(sends, FAR):
        copy.wait()
    for dx, dy in FAR:
        total = total + ret_in[target_slot(dx, dy)]
    force = pick(total, settle)
    force = force[0:3] + force[3:6]
    fresh = held[0:3] + 0.5 * TIME_STEP * force * held[6:7]
    nv_ref[0, 0] = fresh[:, 0:atoms]
    ntr_ref[0, 0] = held[3:6, 0:atoms]


def on_device(*args):
    atoms = args[0].shape[3]
    slots = args[4].shape[2]
    ch = args[13].shape[0]
    chunks = (atoms // GROUP * (slots // 8) + 7) // 8
    n_gx, n_yz = lax.axis_size("gx"), lax.axis_size("yz")
    period = (n_gx * PX * SPACING, n_yz * PY * SPACING, PZ * SPACING)
    args = args[:15] + (args[15].reshape(1, ch),)

    def body(*refs):
        kernel_body(period, atoms, slots, *refs)

    vmem = pl.BlockSpec(memory_space=pltpu.VMEM)
    smem = pl.BlockSpec(memory_space=pltpu.SMEM)
    per_block = slots // 8
    dma = pltpu.SemaphoreType.DMA
    out = jax.ShapeDtypeStruct((1, 1, 3, atoms), F32)
    return pl.pallas_call(
        body,
        out_shape=(out, out),
        in_specs=[vmem] * 8 + [smem] * 2 + [vmem] * 6,
        out_specs=(vmem, vmem),
        scratch_shapes=[
            pltpu.VMEM((9, 8, LANES), F32),
            pltpu.VMEM((3, 8, LANES), F32),
            pltpu.VMEM((15, 8, LANES), F32),
            pltpu.VMEM((15, 8, LANES), F32),
            pltpu.VMEM((slots, LANES), F32),
            pltpu.VMEM((chunks * 8, LANES), F32),
            pltpu.VMEM((4, 8, LANES), F32),
            pltpu.VMEM((13, chunks, 8, LANES), F32),
            pltpu.VMEM((chunks * 128, LANES), F32),
            pltpu.VMEM((chunks * 128, LANES), F32),
            pltpu.VMEM((chunks * 192, LANES), F32),
            pltpu.VMEM((chunks * 64 + 64, LANES), F32),
            pltpu.VMEM((atoms // GROUP, ch, LANES), F32),
            pltpu.VMEM((8, ch, 3 * ch), BF16),
            pltpu.VMEM((ch, 48), BF16),
            pltpu.VMEM((ch, LANES), F32),
            pltpu.VMEM((per_block, ch, LANES), F32),
            pltpu.VMEM((per_block, ch, LANES), F32),
            pltpu.VMEM((per_block, ch, LANES), F32),
            pltpu.VMEM((per_block, ch, LANES), F32),
            pltpu.VMEM((per_block, ch, LANES), F32),
            pltpu.VMEM((9, ch, LANES), F32),
            pltpu.VMEM((9, ch, LANES), F32),
            pltpu.VMEM((3, 64, LANES), F32),
            dma((9,)),
            dma((9,)),
            dma((3,)),
            dma((3,)),
            dma((15,)),
            dma((15,)),
        ],
        compiler_params=pltpu.CompilerParams(
            collective_id=0, has_side_effects=True, vmem_limit_bytes=32 * 1024 * 1024
        ),
    )(*args)


def solution(mesh):
    block4 = P("gx", "yz", None, None)
    block3 = P("gx", "yz", None)
    return jax.shard_map(
        on_device,
        mesh=mesh,
        in_specs=(block4, block4, block4, block3) + (block4,) * 6 + (P(),) * 6,
        out_specs=(block4, block4),
        check_vma=False,
    )
```

profile of v0, /device:TPU:8, one launch (start us, length us, event | category | flops | bytes accessed | tf_op | source)
XLA Modules:
  0.0 41.8 jit_solution(15800806654508493826)
XLA Ops:
  0.6 0.7 %copy.18.refs_0_ = f32[1,1,3,80]{3,2,1,0:T(4,128)S(1)} copy(f32[1,1,3,80]{3,1,2,0:T(1,128)} %param.16) | data formatting | bytes 1920 | tf_op args[0]
  1.3 0.7 %copy.19.refs_1_ = f32[1,1,3,80]{3,2,1,0:T(4,128)S(1)} copy(f32[1,1,3,80]{3,1,2,0:T(1,128)} %param.17) | data formatting | bytes 1920 | tf_op args[1]
  2.0 0.7 %copy.20.refs_2_ = f32[1,1,3,80]{3,2,1,0:T(4,128)S(1)} copy(f32[1,1,3,80]{3,1,2,0:T(1,128)} %param.18) | data formatting | bytes 1920 | tf_op args[2]
  2.7 0.8 %copy.23.refs_11_ = f32[32,5]{1,0:T(8,128)S(1)} copy(f32[32,5]{0,1:T(8,128)} %param.27) | data formatting | bytes 1280 | tf_op args[11]
  3.5 0.8 %copy.24.refs_12_ = f32[32,5]{1,0:T(8,128)S(1)} copy(f32[32,5]{0,1:T(8,128)} %param.28) | data formatting | bytes 1280 | tf_op args[12]
  4.2 0.1 copy.21.refs_4_
  4.3 0.7 %copy-done.9 = s32[1,1,96,80]{2,3,1,0:T(8,128)S(1)} copy-done((s32[1,1,96,80]{2,3,1,0:T(8,128)S(1)}, s32[1,1,96,80]{2,3,1,0:T(8,128)}, u32[]{:S(2)}) %copy-start.9) | copy-done | bytes 30744
  5.0 0.1 copy.22.refs_5_
  5.1 0.6 %copy-done.10 = f32[128,32]{0,1:T(8,128)S(1)} copy-done((f32[128,32]{0,1:T(8,128)S(1)}, f32[128,32]{0,1:T(8,128)}, u32[]{:S(2)}) %copy-start.10) | copy-done | bytes 16408
  5.7 0.0 copy-start.4
  5.8 0.0 copy-start.5
  5.8 0.0 copy-start.6
  5.8 0.0 copy-start.7
  5.8 0.1 copy.25.refs_14_
  5.9 0.6 %copy-done = f32[32,32]{1,0:T(8,128)S(1)} copy-done((f32[32,32]{1,0:T(8,128)S(1)}, f32[32,32]{1,0:T(8,128)}, u32[]{:S(2)}) %copy-start) | copy-done | bytes 4120
  6.4 0.0 copy-done.1
  6.5 0.0 copy-done.3
  6.5 0.0 copy-done.4
  6.5 0.0 copy-done.5
  6.5 0.0 copy-done.6
  6.5 0.0 copy-done.7
  6.5 34.2 %shard_map.167 = (f32[1,1,3,80]{3,2,1,0:T(4,128)S(1)}, f32[1,1,3,80]{3,2,1,0:T(4,128)S(1)}) custom-call(f32[1,1,3,80]{3,2,1,0:T(4,128)S(1)} %copy.18.refs_0_, f32[1,1,3,80]{3,2,1,0:T(4,128)S(1)} %copy.19.refs_1_, f32[1,1,3,80]{3,2,1,0:T(4,128)S(1)} %copy.20.refs_2_, s32[1,1,80]{2,1,0:T(1,128)S(1)} %copy-done.6, s32[1,1,96,80]{3,2,1,0:T(8,128)S(1)} %copy.21.refs_4_, ...), custom_call_target="tpu_custom_call" | custom-call | tf_op jit(solution)/shard_map/pallas_call | solution.py:593
  40.7 0.6 %copy.26 = f32[1,1,3,80]{3,1,2,0:T(1,128)} copy(f32[1,1,3,80]{3,2,1,0:T(4,128)S(1)} %get-tuple-element.2) | data formatting | bytes 1920 | tf_op jit(solution)/shard_map/pallas_call | solution.py:593
  41.2 0.6 %copy.27 = f32[1,1,3,80]{3,1,2,0:T(1,128)} copy(f32[1,1,3,80]{3,2,1,0:T(4,128)S(1)} %get-tuple-element.3) | data formatting | bytes 1920 | tf_op jit(solution)/shard_map/pallas_call | solution.py:593
  (9 shorter events, 0.0 us)
Async XLA Ops:
  0.6 3.6 %copy-start.8 = (s32[1,1,96,80]{2,3,1,0:T(8,128)S(1)}, s32[1,1,96,80]{2,3,1,0:T(8,128)}, u32[]{:S(2)}) copy-start(s32[1,1,96,80]{2,3,1,0:T(8,128)} %param.20) | copy-start | bytes 92164
  4.2 0.8 %copy-start.9 = (s32[1,1,96,80]{2,3,1,0:T(8,128)S(1)}, s32[1,1,96,80]{2,3,1,0:T(8,128)}, u32[]{:S(2)}) copy-start(s32[1,1,96,80]{2,3,1,0:T(8,128)} %param.21) | copy-start | bytes 92164
  5.0 0.7 %copy-start.10 = (f32[128,32]{0,1:T(8,128)S(1)}, f32[128,32]{0,1:T(8,128)}, u32[]{:S(2)}) copy-start(f32[128,32]{0,1:T(8,128)} %param.30) | copy-start | bytes 49156
  5.7 0.7 %copy-start = (f32[32,32]{1,0:T(8,128)S(1)}, f32[32,32]{1,0:T(8,128)}, u32[]{:S(2)}) copy-start(f32[32,32]{1,0:T(8,128)} %refs_13_.1) | copy-start | bytes 12292
  5.7 0.7 %copy-start.1 = (f32[8,32]{1,0:T(8,128)S(1)}, f32[8,32]{1,0:T(8,128)}, u32[]{:S(2)}) copy-start(f32[8,32]{1,0:T(8,128)} %refs_10_.1) | copy-start | bytes 3076
  5.7 0.7 %copy-start.2 = (s32[1,1,2,40]{3,2,1,0:T(2,128)S(1)}, s32[1,1,2,40]{3,2,1,0:T(2,128)}, u32[]{:S(2)}) copy-start(s32[1,1,2,40]{3,2,1,0:T(2,128)} %refs_6_.1) | copy-start | bytes 964
  5.7 0.7 %copy-start.3 = (s32[1,1,2,80]{3,2,1,0:T(2,128)S(1)}, s32[1,1,2,80]{3,2,1,0:T(2,128)}, u32[]{:S(2)}) copy-start(s32[1,1,2,80]{3,2,1,0:T(2,128)} %refs_7_.1) | copy-start | bytes 1924
  5.7 0.7 %copy-start.4 = (s32[1,1,2,5]{3,2,1,0:T(2,128)S(1)}, s32[1,1,2,5]{3,2,1,0:T(2,128)}, u32[]{:S(2)}) copy-start(s32[1,1,2,5]{3,2,1,0:T(2,128)} %refs_8_.1) | copy-start | bytes 124
  5.8 0.7 %copy-start.5 = (s32[1,1,2,5]{3,2,1,0:T(2,128)S(1)}, s32[1,1,2,5]{3,2,1,0:T(2,128)}, u32[]{:S(2)}) copy-start(s32[1,1,2,5]{3,2,1,0:T(2,128)} %refs_9_.1) | copy-start | bytes 124
  5.8 0.7 %copy-start.6 = (s32[1,1,80]{2,1,0:T(1,128)S(1)}, s32[1,1,80]{2,1,0:T(1,128)}, u32[]{:S(2)}) copy-start(s32[1,1,80]{2,1,0:T(1,128)} %refs_3_.1) | copy-start | bytes 964
  5.8 0.7 %copy-start.7 = (f32[32]{0:T(128)S(1)}, f32[32]{0:T(128)}, u32[]{:S(2)}) copy-start(f32[32]{0:T(128)} %param.31) | copy-start | bytes 388
where the time goes:
time: 42.2 us; the launch traced here: 41.8 us
  Pallas kernels  34.2 us (81%)
  local copies, waits for them, and re-layouts  6.93 us (16%)
  between operations  0.71 us (2%)
    pallas_call x1, Pallas kernels, on_device(): pl.pallas_call(body, out_shape=(out, out), in_specs=[vmem] * 8 + [smem] *...  34.2 us
    unnamed x30, local copies, waits for them, and re-layouts  5.8 us
    pallas_call x2, local copies, waits for them, and re-layouts, on_device(): pl.pallas_call(body, out_shape=(out, out), in_specs=[vmem] * 8 + [smem] *...  1.13 us

commit v1 on v0

--- a/solution.py
+++ b/solution.py
@@ -72,68 +72,51 @@
 
 
 def sigmoid(x):
-    return 1.0 / (1.0 + jnp.exp(-x))
-
-
-def lanes_total(x):
-    for shift in (64, 32, 16):
-        x = x + pltpu.roll(x, shift, 1)
-    return x
+    return 0.5 * jnp.tanh(0.5 * x) + 0.5
 
 
 def kernel_body(
     period,
     atoms,
     slots,
-    pos_ref,
-    vel_ref,
-    frc_ref,
-    spc_ref,
-    nbr_ref,
-    msk_ref,
-    sx_ref,
-    sy_ref,
-    ms_ref,
-    mr_ref,
-    wb_ref,
-    ec_ref,
-    en_ref,
-    we_ref,
-    wl_ref,
-    wo_ref,
-    nv_ref,
-    ntr_ref,
-    halo,
-    load,
-    ret_out,
-    ret_in,
-    nb_pad,
-    rows_code,
-    table,
-    sc,
-    zf,
-    zy,
-    zd,
-    pt,
-    cterm,
-    mats,
-    w1s,
-    wcol,
-    pre_s,
-    sig_s,
-    ef_s,
-    dlp_s,
-    hid_s,
-    gs,
-    dfs,
-    g3,
-    halo_send,
-    halo_recv,
-    load_send,
-    load_recv,
-    ret_send,
-    ret_recv,
+    *refs,
 ):
+    raw, refs = refs[:16], refs[16:]
+    (
+        nv_ref,
+        ntr_ref,
+        staged,
+        halo,
+        load,
+        ret_out,
+        ret_in,
+        nb_pad,
+        rows_code,
+        table,
+        sc,
+        zf,
+        zy,
+        zd,
+        pt,
+        cterm,
+        mats,
+        w1s,
+        wcol,
+        w0pad,
+        rhs,
+        s1_s,
+        ds_s,
+        hid_s,
+        dpt_s,
+        g3,
+        load_sems,
+        halo_send,
+        halo_recv,
+        load_send,
+        load_recv,
+        ret_send,
+        ret_recv,
+    ) = refs
     gx = lax.axis_index("gx")
     yz = lax.axis_index("yz")
     n_gx = lax.axis_size("gx")
@@ -150,6 +133,33 @@
     for dx, dy in FAR:
         pl.semaphore_signal(barrier, inc=1, device_id=device(dx, dy), device_id_type=MESH)
 
+    loads = []
+    for at, (far, close) in enumerate(zip(raw, staged)):
+        copy = pltpu.make_async_copy(far, close, load_sems.at[at])
+        copy.start()
+        loads.append(copy)
+    (
+        pos_ref,
+        vel_ref,
+        frc_ref,
+        spc_ref,
+        nbr_ref,
+        msk_ref,
+        sx_ref,
+        sy_ref,
+        ms_ref,
+        mr_ref,
+        wb_ref,
+        ec_ref,
+        en_ref,
+        we_ref,
+        wl_ref,
+        wo_ref,
+    ) = staged
+    first = (0, 1, 2, 3, 6, 7, 8, 9)
+    for at in first:
+        loads[at].wait()
+
     lane1 = lax.broadcasted_iota(I32, (1, LANES), 1)
     lane8 = lax.broadcasted_iota(I32, (8, LANES), 1)
     sub8 = lax.broadcasted_iota(I32, (8, LANES), 0)
@@ -159,13 +169,15 @@
     minv = jnp.zeros_like(kinds)
     for kind, mass in enumerate(MASSES):
         minv = jnp.where(kinds == float(kind), 1.0 / jnp.float32(mass), minv)
-    start = pos_ref[0, 0]
-    velocity = vel_ref[0, 0] + 0.5 * TIME_STEP * frc_ref[0, 0] * minv
-    coords = start + TIME_STEP * velocity
-    travel = (coords - start) / (STEPS * TIME_STEP)
     halo[own] = jnp.zeros((8, LANES), F32)
     load[1] = jnp.zeros((8, LANES), F32)
-    halo[own, 0:3, 0:atoms] = coords
+    for c in range(3):
+        start = pos_ref[0, c]
+        velocity = vel_ref[0, c] + 0.5 * TIME_STEP * frc_ref[0, c] * minv
+        coords = start + TIME_STEP * velocity
+        halo[own, c : c + 1, 0:atoms] = coords
+        load[1, c : c + 1, 0:atoms] = velocity
+        load[1, c + 3 : c + 4, 0:atoms] = (coords - start) / (STEPS * TIME_STEP)
     halo[own, 3:4, 0:atoms] = kinds
     code = lane1
     place = lane1
@@ -187,8 +199,6 @@
     code = jnp.where(lane1 < atoms, code + LANES, 0)
     halo[own, 4:5, :] = code.astype(F32)
     halo[own, 6:8, 0:atoms] = sy_ref[0, 0].astype(F32)
-    load[1, 0:3, 0:atoms] = velocity
-    load[1, 3:6, 0:atoms] = travel
     load[1, 6:7, 0:atoms] = minv
     width_x = sx_ref.shape[3]
     g3[0] = jnp.zeros((64, LANES), F32)
@@ -224,15 +234,21 @@
         copy.start()
         sends.append(copy)
 
-    nb_pad[...] = jnp.zeros((slots, LANES), F32)
-    nb_pad[:, 0:atoms] = nbr_ref[0, 0].astype(F32) + 512.0 * msk_ref[0, 0].astype(F32)
+    for at in range(16):
+        if at not in first:
+            loads[at].wait()
+    nb_pad[...] = jnp.zeros((atoms, LANES), F32)
+    nb_pad[:, 0:slots] = nbr_ref[0, 0].astype(F32) + 512.0 * msk_ref[0, 0].astype(F32)
     rows_code[...] = jnp.zeros((chunks * 8, LANES), F32)
-    in_group = lane8 // GROUP == sub8
+    atom_of_lane = lane8 & (GROUP - 1)
+    in_row = (lane8 & 7) == sub8
     for block in range(blocks):
-        spread = (lane8 & (GROUP - 1)) + block * GROUP
+        upper = nb_pad[block * GROUP : block * GROUP + 8, :]
+        lower = nb_pad[block * GROUP + 8 : block * GROUP + 16, :]
         for jb in range(per_block):
-            moved = pick(nb_pad[jb * 8 : jb * 8 + 8, :], spread)
-            row = jnp.sum(jnp.where(in_group, moved, 0.0), axis=0, keepdims=True)
+            slot = (lane8 >> 4) + jb * 8
+            moved = jnp.where(atom_of_lane < 8, pick(upper, slot), pick(lower, slot))
+            row = jnp.sum(jnp.where(in_row, moved, 0.0), axis=0, keepdims=True)
             r = block * per_block + jb
             rows_code[r : r + 1, :] = row
 
@@ -240,24 +256,44 @@
     eye = (
         lax.broadcasted_iota(I32, (ch, ch), 0) == lax.broadcasted_iota(I32, (ch, ch), 1)
     ).astype(F32)
+    n_basis = wb_ref.shape[0]
+    n_kinds = en_ref.shape[0]
+    wl_t = wl_ref[...]
+    mixes = []
     for part in range(3):
-        mixed = ENV_SCALE * nn_dot(we_ref[...], wl_ref[(part + 1) * ch : (part + 2) * ch, :], HIGHEST)
-        mats[2 + part] = left_parts(nt_dot(eye, mixed, HIGHEST))
-        mats[5 + part] = left_parts(mixed)
-    mats[0] = left_parts(nt_dot(eye, wl_ref[0:ch, :], HIGHEST))
-    mats[1] = left_parts(wl_ref[0:ch, :])
-    n_basis = wb_ref.shape[0]
-    n_kinds = en_ref.shape[1]
+        part_t = wl_t[:, (part + 1) * ch : (part + 2) * ch]
+        mixes.append(ENV_SCALE * nt_dot(part_t, we_ref[...], HIGHEST))
+    for part in range(3):
+        turned = mixes[part]
+        straight = nt_dot(eye, turned, HIGHEST)
+        for which, m in enumerate((straight, turned)):
+            m_high, m_low = halves(m)
+            mats[which, 0, part] = m_high
+            mats[which, 1, part] = m_low
+    w0_t = wl_t[:, 0:ch]
+    w0 = nt_dot(eye, w0_t, HIGHEST)
+    ec = nt_dot(eye, ec_ref[...], HIGHEST)
+    w0pad[...] = jnp.zeros((2, ch, LANES), F32)
+    w0pad[0, :, GROUP : GROUP + ch] = w0_t
+    w0pad[1, :, GROUP + ch : GROUP + 2 * ch] = w0
     w1f = jnp.concatenate(
         [
             nt_dot(eye, wb_ref[...], HIGHEST),
-            en_ref[...],
+            nt_dot(eye, en_ref[...], HIGHEST),
             jnp.zeros((ch, 16 - n_basis - n_kinds), F32),
         ],
         axis=1,
     )
     w1s[...] = left_parts(w1f)
-    w_basis = left_parts(wb_ref[...])
+    row32 = lax.broadcasted_iota(I32, (32, LANES), 0)
+    lane32 = lax.broadcasted_iota(I32, (32, LANES), 1)
+    g3[1, 0:32, :] = jnp.zeros((32, LANES), F32)
+    g3[1, 0:n_basis, 0:ch] = wb_ref[...]
+    head = g3[1, 0:32, :] + jnp.where(
+        (row32 == 8) & (lane32 >= ch) & (lane32 < 2 * ch), 1.0, 0.0
+    ) + jnp.where((lane32 >= 2 * ch) & (row32 == 16 + ((lane32 - 2 * ch) >> 4)), 1.0, 0.0)
+    rest = jnp.where(row32 == 16 + ((lane32 + LANES - 2 * ch) >> 4), 1.0, 0.0)
+    w_last = jnp.concatenate([head, rest], axis=1).astype(BF16)[:, 0 : 2 * ch + LANES]
     wcol[...] = jnp.broadcast_to(
         jnp.sum(jnp.where(eye > 0, wo_ref[...], 0.0), axis=1, keepdims=True), (ch, LANES)
     )
@@ -299,7 +335,7 @@
         return jnp.broadcast_to(table[k, c : c + 1, :], (8, LANES))
 
     def forward_chunk(i, carry):
-        word = rows_code[pl.ds(pl.multiple_of(i * 8, 8), 8), :]
+        word = rows_code[pl.ds(i * 8, 8), :]
         live = word >= 512.0
         n = jnp.where(live, word - 512.0, word).astype(I32)
         k = jnp.where(n >= atoms, 1, 0) + jnp.where(n >= 2 * atoms, 1, 0) + jnp.where(n >= 3 * atoms, 1, 0)
@@ -372,7 +408,8 @@
         pt[pl.ds(tbase + 7, 8, stride=8), :] = (dest & (LANES - 1)).astype(F32)
         return carry
 
-    lax.fori_loop(0, chunks, forward_chunk, 0)
+    for i in range(chunks):
+        forward_chunk(i, 0)
 
     for block in range(blocks):
         spread = (lane8 & (GROUP - 1)) + block * GROUP
@@ -381,88 +418,119 @@
         for kind in range(n_kinds):
             term = jnp.where(
                 kind_row == float(kind),
-                jnp.broadcast_to(ec_ref[:, kind : kind + 1], (ch, LANES)),
+                jnp.broadcast_to(ec[:, kind : kind + 1], (ch, LANES)),
                 term,
             )
         cterm[block] = term
 
-    degrees = (0, 1, 1, 1, 2, 2, 2, 2, 2)
-
-    def y_rows(row):
-        return [zy[pl.ds(row * 16 + m, 1), :] for m in range(9)]
-
-    def by_degree(first, parts):
-        out = []
-        for degree, (a, b) in enumerate(((0, 1), (1, 4), (4, 9))):
-            joined = jnp.concatenate(parts[a:b], axis=1)
-            got = nn_dot(mats[first + degree], right_parts(joined))
-            out += [got[:, t * LANES : (t + 1) * LANES] for t in range(b - a)]
-        return out
-
-    def block_body(block, carry):
-        base = block * per_block
+    n_harm = 8
+    wide = n_harm * GROUP
+    own_lane = lax.broadcasted_iota(I32, (GROUP, LANES), 0) == (
+        lax.broadcasted_iota(I32, (GROUP, LANES), 1) & (GROUP - 1)
+    )
+    every = jnp.concatenate([own_lane] * n_harm, axis=0)
+    ones_row = jnp.where(own_lane, 1.0, 0.0).astype(BF16)
+    at_ef = wide + GROUP
+    at_dlp = at_ef + ch
+
+    def by_degree(which, sums):
+        parts = []
+        for degree, (a, b) in ((1, (0, 3)), (2, (3, n_harm)), (0, (n_harm, n_harm + 1))):
+            rows = sums[a * GROUP : b * GROUP]
+            parts.append(exact_dot(rows, which, degree))
+        return jnp.concatenate(parts, axis=0)
+
+    def exact_dot(rows, which, degree):
+        high, low = halves(rows)
+        m_high, m_low = mats[which, 0, degree], mats[which, 1, degree]
+        return nn_dot(high, m_high) + nn_dot(low, m_high) + nn_dot(high, m_low)
+
+    def as_left(turned, pad):
+        tall_one = jnp.concatenate([turned, jnp.zeros((2 * LANES - wide - GROUP, ch), F32)], axis=0)
+        left = tall_one.T
+        return jnp.concatenate([left[:, 0:LANES], left[:, LANES:] + pad], axis=1).astype(BF16)
+
+    w_out = wcol[...]
+    kept = {}
+
+    def env_row(row):
+        return zy[row * 16 + 8 : row * 16 + 9, :]
+
+    def stage_pre(b):
+        base = b * per_block
         feats = jnp.concatenate(
-            [zf[pl.ds(pl.multiple_of((base + jb) * 16, 16), 16), :] for jb in range(per_block)], axis=1
+            [zf[(base + jb) * 16 : (base + jb + 1) * 16, :] for jb in range(per_block)], axis=1
         )
-        pre = nn_dot(w1s[...], right_parts(feats))
-        centre_term = cterm[block]
-        acc = None
+        kept["pre", b] = nn_dot(w1s[...], right_parts(feats))
+
+    def stage_feat(b):
+        centre_term = cterm[b]
+        pre = kept.pop(("pre", b))
         for jb in range(per_block):
-            p = pre[:, jb * LANES : (jb + 1) * LANES] + centre_term
-            *ys, env = y_rows(base + jb)
+            row = b * per_block + jb
+            cols = slice(jb * LANES, (jb + 1) * LANES)
+            z = zy[row * 16 : row * 16 + 16, :]
+            env = z[8:9]
+            p = pre[:, cols] + centre_term
             sig = sigmoid(p)
-            ef = p * sig * env
-            pre_s[jb] = p
-            sig_s[jb] = sig
-            ef_s[jb] = ef
-            new = [ef] + [ef * y for y in ys]
-            acc = new if acc is None else [a + b for a, b in zip(acc, new)]
-        sums = [lanes_total(a) for a in acc]
-        grow = by_degree(2, sums)
-        for m in range(9):
-            gs[m] = grow[m]
-        mixed = nn_dot(mats[0], right_parts(jnp.concatenate([ef_s[jb] for jb in range(per_block)], axis=1)))
-        acc = None
-        w_out = wcol[...]
+            s1 = p * sig
+            s1_s[row] = s1
+            ds_s[row] = (sig + s1 * (1.0 - sig)) * env
+            rhs[b, at_ef : at_ef + ch, cols] = (s1 * env).astype(BF16)
+            for m in range(n_harm):
+                rhs[b, m * GROUP : (m + 1) * GROUP, cols] = jnp.where(own_lane, z[m : m + 1], 0.0).astype(BF16)
+            rhs[b, wide : wide + GROUP, cols] = ones_row
+
+    def stage_env(b):
+        sums = nt_dot(rhs[b, 0:at_ef, :], rhs[b, at_ef : at_ef + ch, :])
+        grown = by_degree(0, sums)
+        kept["g", b] = grown[0:wide]
+        left = as_left(grown, w0pad[0])
+        kept["lp", b] = nn_dot(left[:, 0:at_dlp], rhs[b, 0:at_dlp, :])
+
+    def stage_latent(b):
+        lp_all = kept.pop(("lp", b))
         for jb in range(per_block):
-            *ys, env = y_rows(base + jb)
-            lp = mixed[:, jb * LANES : (jb + 1) * LANES] + gs[0]
-            for m in range(8):
-                lp = lp + gs[m + 1] * ys[m]
+            row = b * per_block + jb
+            cols = slice(jb * LANES, (jb + 1) * LANES)
+            env = env_row(row)
+            lp = lp_all[:, cols]
             sig = sigmoid(lp)
             lat = lp * sig
-            hid_s[jb] = w_out * (ef_s[jb] + lat)
+            hid_s[row] = w_out * (s1_s[row] * env + lat)
             dlp = (w_out * env) * (sig + lat * (1.0 - sig))
-            dlp_s[jb] = dlp
-            new = [dlp] + [dlp * y for y in ys]
-            acc = new if acc is None else [a + b for a, b in zip(acc, new)]
-        sums = [lanes_total(a) for a in acc]
-        grow = by_degree(5, sums)
-        for m in range(9):
-            dfs[m] = grow[m]
-        mixed = nn_dot(mats[1], right_parts(jnp.concatenate([dlp_s[jb] for jb in range(per_block)], axis=1)))
-        dps = []
+            rhs[b, at_dlp : at_dlp + ch, cols] = dlp.astype(BF16)
+
+    def stage_back(b):
+        sums = nt_dot(rhs[b, 0:at_ef, :], rhs[b, at_dlp : at_dlp + ch, :])
+        grown = by_degree(1, sums)
+        left = as_left(grown, w0pad[1])
+        kept["de", b] = nn_dot(left[:, 0 : at_dlp + ch], rhs[b])
+        both = jnp.concatenate([grown[0:wide], kept.pop(("g", b))], axis=1).astype(BF16)
+        kept["dy", b] = nn_dot(both, rhs[b, at_ef : at_dlp + ch, :])
+
+    def stage_edge(b):
+        de_all = kept.pop(("de", b))
+        dy_all = kept.pop(("dy", b))
         for jb in range(per_block):
-            *ys, env = y_rows(base + jb)
-            de = mixed[:, jb * LANES : (jb + 1) * LANES] + w_out * env + dfs[0]
-            for m in range(8):
-                de = de + dfs[m + 1] * ys[m]
-            sig = sig_s[jb]
-            s1 = pre_s[jb] * sig
-            dps.append(de * env * (sig + s1 * (1.0 - sig)))
-            zbase = (base + jb) * 24
-            zd[pl.ds(zbase + 16, 1), :] = jnp.sum(hid_s[jb] + de * s1, axis=0, keepdims=True)
-            ef, dlp = ef_s[jb], dlp_s[jb]
-            for m in range(8):
-                zd[pl.ds(zbase + 8 + m, 1), :] = jnp.sum(
-                    gs[m + 1] * dlp + dfs[m + 1] * ef, axis=0, keepdims=True
-                )
-        dbes = nn_dot(w_basis, right_parts(jnp.concatenate(dps, axis=1)))
+            row = b * per_block + jb
+            cols = slice(jb * LANES, (jb + 1) * LANES)
+            de = de_all[:, cols] + w_out * env_row(row)
+            dpt_s[b, 0:ch, cols] = (de * ds_s[row]).astype(BF16)
+            dpt_s[b, ch : 2 * ch, cols] = (hid_s[row] + de * s1_s[row]).astype(BF16)
+            dpt_s[b, 2 * ch :, cols] = jnp.where(every, dy_all[:, cols], 0.0).astype(BF16)
+
+    def stage_fold(b):
+        got = nn_dot(w_last, dpt_s[b])
         for jb in range(per_block):
-            zd[pl.ds(pl.multiple_of((base + jb) * 24, 8), 8), :] = dbes[:, jb * LANES : (jb + 1) * LANES]
-        return carry
-
-    lax.fori_loop(0, blocks, block_body, 0)
+            row = b * per_block + jb
+            zd[row * 24 : row * 24 + 24, :] = got[0:24, jb * LANES : (jb + 1) * LANES]
+
+    stages = (stage_pre, stage_feat, stage_env, stage_latent, stage_back, stage_edge, stage_fold)
+    for tick in range(len(stages) + blocks - 1):
+        for b in range(blocks):
+            if 0 <= tick - b < len(stages):
+                stages[tick - b](b)
     for row in range(n_rows, chunks * 8):
         zd[row * 24 : row * 24 + 24, :] = jnp.zeros((24, LANES), F32)
 
@@ -479,16 +547,16 @@
             return zd[pl.ds(zbase + which, 8, stride=24), :]
 
         ux, uy, uz, rinv, denv = (sc[t, i] for t in range(5))
-        dr = d(16) * denv
+        dr = d(8) * denv
         for order in range(n_basis):
             dr = dr + d(order) * sc[5 + order, i]
-        d1, d2, d3, d4, d5, d6, d7, d8 = (d(8 + m) for m in range(8))
+        d1, d2, d3, d4, d5, d6, d7, d8 = (d(16 + m) for m in range(8))
         dux = R3 * d1 + R15 * (uy * d4 + uz * d7 + ux * d8)
         duy = R3 * d2 + R15 * (ux * d4 + uz * d5 - uy * d8)
         duz = R3 * d3 + R15 * (uy * d5 + ux * d7) + (3.0 * R5) * uz * d6
         radial = dr - rinv * (dux * ux + duy * uy + duz * uz)
         forces = [-(radial * u + rinv * du) for u, du in ((ux, dux), (uy, duy), (uz, duz))]
-        at = pl.ds(pl.multiple_of(i * 8, 8), 8)
+        at = pl.ds(i * 8, 8)
         for c in range(3):
             g3[c, at, :] = forces[c]
 
@@ -498,7 +566,8 @@
         put_parts(store, forces)
         return carry
 
-    lax.fori_loop(0, chunks, backward_chunk, 0)
+    for i in range(chunks):
+        backward_chunk(i, 0)
 
     extra = chunks * 8
     pt[extra * 8 :, :] = jnp.zeros((8 * 8, LANES), F32)
@@ -520,23 +589,28 @@
 
     n_targets = len(TARGETS)
     tall = 96
-    sub_tall = lax.broadcasted_iota(I32, (tall, LANES), 0).astype(F32)
+    sub16 = lax.broadcasted_iota(I32, (16, LANES), 0)
+    pair = jnp.where(sub16 >= 8, 1.0, 0.0)
+    pairs = [(pair + 2.0 * b).astype(BF16) for b in range((n_targets + 1) // 2)]
+    steps = [(sub16 + 16 * b).astype(F32).astype(BF16) for b in range(tall // 16)]
+    zero16 = jnp.zeros((16, LANES), BF16)
+    one16 = jnp.ones((16, LANES), BF16)
 
     def scatter_body(i, acc):
         lefts, rights = [], []
         for t in range(8):
             v = pt[pl.ds(pl.multiple_of((i * 8 + t) * 8, 8), 8), :]
-            where_to, lo = v[6:7], v[7:8]
-            lefts.append(
-                jnp.concatenate([jnp.where(where_to == float(b), v, 0.0) for b in range(n_targets)], axis=0)
-            )
-            rights.append(jnp.where(lo == sub_tall, 1.0, 0.0))
-        left = jnp.concatenate(lefts, axis=1).astype(BF16)
-        right = jnp.concatenate(rights, axis=1).astype(BF16)
+            where_to = jnp.broadcast_to(v[6:7], (16, LANES)).astype(BF16)
+            lo = jnp.broadcast_to(v[7:8], (16, LANES)).astype(BF16)
+            twice = jnp.concatenate([v, v], axis=0).astype(BF16)
+            lefts.append(jnp.concatenate([jnp.where(where_to == p, twice, zero16) for p in pairs], axis=0))
+            rights.append(jnp.concatenate([jnp.where(lo == p, one16, zero16) for p in steps], axis=0))
+        left = jnp.concatenate(lefts, axis=1)
+        right = jnp.concatenate(rights, axis=1)
         return acc + nt_dot(left, right)
 
     spread_out = lax.fori_loop(
-        0, chunks + 1, scatter_body, jnp.zeros((n_targets * 8, tall), F32)
+        0, chunks + 1, scatter_body, jnp.zeros((len(pairs) * 16, tall), F32)
     )
     for t in range(n_targets):
         ret_out[t] = jnp.zeros((8, LANES), F32)
@@ -569,8 +643,9 @@
     force = pick(total, settle)
     force = force[0:3] + force[3:6]
     fresh = held[0:3] + 0.5 * TIME_STEP * force * held[6:7]
-    nv_ref[0, 0] = fresh[:, 0:atoms]
-    ntr_ref[0, 0] = held[3:6, 0:atoms]
+    for c in range(3):
+        nv_ref[0, c] = fresh[c : c + 1, 0:atoms]
+        ntr_ref[0, c] = held[c + 3 : c + 4, 0:atoms]
 
 
 def on_device(*args):
@@ -580,27 +655,34 @@
     chunks = (atoms // GROUP * (slots // 8) + 7) // 8
     n_gx, n_yz = lax.axis_size("gx"), lax.axis_size("yz")
     period = (n_gx * PX * SPACING, n_yz * PY * SPACING, PZ * SPACING)
-    args = args[:15] + (args[15].reshape(1, ch),)
+    pos, vel, frc, spc, nbr, msk, sx, sy, ms, mr, wb, ec, en, we, wl, wo = args
+    pos, vel, frc = (x.transpose(0, 2, 1, 3) for x in (pos, vel, frc))
+    nbr, msk = (x.transpose(0, 1, 3, 2) for x in (nbr, msk))
+    args = (pos, vel, frc, spc, nbr, msk, sx, sy, ms, mr, wb, ec.T, en.T, we, wl.T, wo.reshape(1, ch))
 
     def body(*refs):
         kernel_body(period, atoms, slots, *refs)
 
     vmem = pl.BlockSpec(memory_space=pltpu.VMEM)
-    smem = pl.BlockSpec(memory_space=pltpu.SMEM)
     per_block = slots // 8
+    blocks = atoms // GROUP
     dma = pltpu.SemaphoreType.DMA
-    out = jax.ShapeDtypeStruct((1, 1, 3, atoms), F32)
-    return pl.pallas_call(
+    out = jax.ShapeDtypeStruct((1, 3, 1, atoms), F32)
+    staged = tuple(
+        (pltpu.SMEM if at in (8, 9) else pltpu.VMEM)(x.shape, x.dtype) for at, x in enumerate(args)
+    )
+    velocity, travel = pl.pallas_call(
         body,
         out_shape=(out, out),
-        in_specs=[vmem] * 8 + [smem] * 2 + [vmem] * 6,
+        in_specs=[pl.BlockSpec(memory_space=pl.ANY)] * 16,
         out_specs=(vmem, vmem),
         scratch_shapes=[
+            staged,
             pltpu.VMEM((9, 8, LANES), F32),
             pltpu.VMEM((3, 8, LANES), F32),
             pltpu.VMEM((15, 8, LANES), F32),
             pltpu.VMEM((15, 8, LANES), F32),
-            pltpu.VMEM((slots, LANES), F32),
+            pltpu.VMEM((atoms, LANES), F32),
             pltpu.VMEM((chunks * 8, LANES), F32),
             pltpu.VMEM((4, 8, LANES), F32),
             pltpu.VMEM((13, chunks, 8, LANES), F32),
@@ -609,17 +691,17 @@
             pltpu.VMEM((chunks * 192, LANES), F32),
             pltpu.VMEM((chunks * 64 + 64, LANES), F32),
             pltpu.VMEM((atoms // GROUP, ch, LANES), F32),
-            pltpu.VMEM((8, ch, 3 * ch), BF16),
+            pltpu.VMEM((2, 2, 3, ch, ch), BF16),
             pltpu.VMEM((ch, 48), BF16),
             pltpu.VMEM((ch, LANES), F32),
-            pltpu.VMEM((per_block, ch, LANES), F32),
-            pltpu.VMEM((per_block, ch, LANES), F32),
-            pltpu.VMEM((per_block, ch, LANES), F32),
-            pltpu.VMEM((per_block, ch, LANES), F32),
-            pltpu.VMEM((per_block, ch, LANES), F32),
-            pltpu.VMEM((9, ch, LANES), F32),
-            pltpu.VMEM((9, ch, LANES), F32),
+            pltpu.VMEM((2, ch, LANES), F32),
+            pltpu.VMEM((blocks, 9 * GROUP + 2 * ch, per_block * LANES), BF16),
+            pltpu.VMEM((blocks * per_block, ch, LANES), F32),
+            pltpu.VMEM((blocks * per_block, ch, LANES), F32),
+            pltpu.VMEM((blocks * per_block, ch, LANES), F32),
+            pltpu.VMEM((blocks, 2 * ch + 8 * GROUP, per_block * LANES), BF16),
             pltpu.VMEM((3, 64, LANES), F32),
+            dma((16,)),
             dma((9,)),
             dma((9,)),
             dma((3,)),
@@ -628,9 +710,10 @@
             dma((15,)),
         ],
         compiler_params=pltpu.CompilerParams(
-            collective_id=0, has_side_effects=True, vmem_limit_bytes=32 * 1024 * 1024
+            collective_id=0, has_side_effects=True, vmem_limit_bytes=60 * 1024 * 1024
         ),
     )(*args)
+    return velocity.transpose(0, 2, 1, 3), travel.transpose(0, 2, 1, 3)
 
 
 def solution(mesh):

time: 42.2 us -> 34.4 us (0.82)
  local copies, waits for them, and re-layouts: 6.93 us -> 1.85 us
  Pallas kernels: 34.2 us -> 31.7 us
    unnamed x30 -> x6, local copies, waits for them, and re-layouts: 5.8 us -> 1.85 us
    pallas_call x1, Pallas kernels: 34.2 us -> 31.7 us  [on_device(): pl.pallas_call(body, out_shape=(out, out), in_specs=[pl.BlockSpec(memory_...]
    pallas_call x2 -> x0, local copies, waits for them, and re-layouts: 1.13 us -> none  [on_device(): pl.pallas_call(body, out_shape=(out, out), in_specs=[vmem] * 8 + [smem] *...]
where the time goes in v1:
time: 34.4 us; the launch traced here: 34.2 us
  Pallas kernels  31.7 us (92%)
  local copies, waits for them, and re-layouts  1.85 us (5%)
  between operations  0.65 us (2%)
    pallas_call x1, Pallas kernels, on_device(): pl.pallas_call(body, out_shape=(out, out), in_specs=[pl.BlockSpec(memory_...  31.7 us
    unnamed x6, local copies, waits for them, and re-layouts  1.85 us

profile of v1, /device:TPU:8, one launch (start us, length us, event | category | flops | bytes accessed | tf_op | source)
XLA Modules:
  0.0 34.2 jit_solution(4766922220240281469)
XLA Ops:
  0.6 31.7 %shard_map.167 = (f32[1,3,1,80]{3,2,1,0:T(1,128)}, f32[1,3,1,80]{3,2,1,0:T(1,128)}) custom-call(f32[1,3,1,80]{3,2,1,0:T(1,128)} %bitcast.20, f32[1,3,1,80]{3,2,1,0:T(1,128)} %bitcast.21, f32[1,3,1,80]{3,2,1,0:T(1,128)} %bitcast.22, s32[1,1,80]{2,1,0:T(1,128)} %refs_3_.1, s32[1,1,80,96]{3,2,1,0:T(8,128)} %bitcast.15, s32[1,1,80,96]{3,2,1,0:T(8,128)} %bitcast.16, ...), custom_call_target="tpu_custom_call" | custom-call | tf_op jit(solution)/shard_map/pallas_call | solution.py:674
  32.3 0.0 copy-start.1
  32.3 0.7 %copy-done.1 = f32[1,3,1,80]{3,2,1,0:T(1,128)S(1)} copy-done((f32[1,3,1,80]{3,2,1,0:T(1,128)S(1)}, f32[1,3,1,80]{3,2,1,0:T(1,128)}, u32[]{:S(2)}) %copy-start.1) | copy-done | bytes 984
  33.0 0.0 copy-start
  33.0 0.6 %copy.22 = f32[1,1,3,80]{3,1,2,0:T(1,128)} copy(f32[1,1,3,80]{3,1,2,0:T(1,128)S(1)} %bitcast.24) | data formatting | bytes 1920
  33.5 0.1 copy-done
  33.6 0.6 %copy.23 = f32[1,1,3,80]{3,1,2,0:T(1,128)} copy(f32[1,1,3,80]{3,1,2,0:T(1,128)S(1)} %bitcast.23) | data formatting | bytes 1920
Async XLA Ops:
  32.3 0.7 %copy-start.1 = (f32[1,3,1,80]{3,2,1,0:T(1,128)S(1)}, f32[1,3,1,80]{3,2,1,0:T(1,128)}, u32[]{:S(2)}) copy-start(f32[1,3,1,80]{3,2,1,0:T(1,128)} %get-tuple-element.4) | copy-start | bytes 2884
  33.0 0.6 %copy-start = (f32[1,3,1,80]{3,2,1,0:T(1,128)S(1)}, f32[1,3,1,80]{3,2,1,0:T(1,128)}, u32[]{:S(2)}) copy-start(f32[1,3,1,80]{3,2,1,0:T(1,128)} %get-tuple-element.5) | copy-start | bytes 2884

commit v2 on v1

--- a/solution.py
+++ b/solution.py
@@ -21,7 +21,7 @@
 I32 = jnp.int32
 
 LANES = 128
-GROUP = 16
+GROUP = 8
 PI = 3.141592653589793
 R3 = 3.0**0.5
 R5 = 5.0**0.5
@@ -57,18 +57,18 @@
     return high, low
 
 
-def left_parts(w):
-    high, low = halves(w)
-    return jnp.concatenate([high, high, low], axis=1)
-
-
-def right_parts(x):
-    high, low = halves(x)
-    return jnp.concatenate([high, low, high], axis=0)
-
-
 def pick(rows, index):
     return jnp.take_along_axis(rows, index, axis=1, mode="promise_in_bounds")
+
+
+def turn(eye, x):
+    high, low = halves(x)
+    return nt_dot(eye, high) + nt_dot(eye, low)
+
+
+def split_dot(left, right):
+    high, low = halves(left)
+    return nn_dot(high, right) + nn_dot(low, right)
 
 
 def sigmoid(x):
@@ -83,8 +83,7 @@
 ):
     raw, refs = refs[:16], refs[16:]
     (
-        nv_ref,
-        ntr_ref,
+        both_ref,
         staged,
         halo,
         load,
@@ -122,7 +121,7 @@
     n_gx = lax.axis_size("gx")
     n_yz = lax.axis_size("yz")
     blocks = atoms // GROUP
-    per_block = slots // 8
+    per_block = slots // 16
     n_rows = blocks * per_block
     chunks = (n_rows + 7) // 8
 
@@ -130,14 +129,18 @@
         return (lax.rem(gx + dx + n_gx, n_gx), lax.rem(yz + dy + n_yz, n_yz))
 
     barrier = pltpu.get_barrier_semaphore()
+    loads = []
+    first = (0, 1, 2, 3, 6, 7, 8, 9)
+    for at, (far, close) in enumerate(zip(raw, staged)):
+        loads.append(pltpu.make_async_copy(far, close, load_sems.at[at]))
+    for at in first:
+        loads[at].start()
     for dx, dy in FAR:
         pl.semaphore_signal(barrier, inc=1, device_id=device(dx, dy), device_id_type=MESH)
 
-    loads = []
-    for at, (far, close) in enumerate(zip(raw, staged)):
-        copy = pltpu.make_async_copy(far, close, load_sems.at[at])
-        copy.start()
-        loads.append(copy)
+    for at in range(16):
+        if at not in first:
+            loads[at].start()
     (
         pos_ref,
         vel_ref,
@@ -156,7 +159,6 @@
         wl_ref,
         wo_ref,
     ) = staged
-    first = (0, 1, 2, 3, 6, 7, 8, 9)
     for at in first:
         loads[at].wait()
 
@@ -240,14 +242,11 @@
     nb_pad[...] = jnp.zeros((atoms, LANES), F32)
     nb_pad[:, 0:slots] = nbr_ref[0, 0].astype(F32) + 512.0 * msk_ref[0, 0].astype(F32)
     rows_code[...] = jnp.zeros((chunks * 8, LANES), F32)
-    atom_of_lane = lane8 & (GROUP - 1)
-    in_row = (lane8 & 7) == sub8
+    in_row = (lane8 & (GROUP - 1)) == sub8
     for block in range(blocks):
-        upper = nb_pad[block * GROUP : block * GROUP + 8, :]
-        lower = nb_pad[block * GROUP + 8 : block * GROUP + 16, :]
+        group = nb_pad[block * GROUP : (block + 1) * GROUP, :]
         for jb in range(per_block):
-            slot = (lane8 >> 4) + jb * 8
-            moved = jnp.where(atom_of_lane < 8, pick(upper, slot), pick(lower, slot))
+            moved = pick(group, (lane8 >> 3) + jb * 16)
             row = jnp.sum(jnp.where(in_row, moved, 0.0), axis=0, keepdims=True)
             r = block * per_block + jb
             rows_code[r : r + 1, :] = row
@@ -260,40 +259,41 @@
     n_kinds = en_ref.shape[0]
     wl_t = wl_ref[...]
     mixes = []
+    eye16 = eye.astype(BF16)
+    we_h, we_l = halves(we_ref[...])
     for part in range(3):
         part_t = wl_t[:, (part + 1) * ch : (part + 2) * ch]
-        mixes.append(ENV_SCALE * nt_dot(part_t, we_ref[...], HIGHEST))
+        part_h, part_l = halves(part_t)
+        mixes.append(ENV_SCALE * (nt_dot(part_h, we_h) + nt_dot(part_l, we_h) + nt_dot(part_h, we_l)))
     for part in range(3):
         turned = mixes[part]
-        straight = nt_dot(eye, turned, HIGHEST)
+        straight = turn(eye16, turned)
         for which, m in enumerate((straight, turned)):
             m_high, m_low = halves(m)
-            mats[which, 0, part] = m_high
-            mats[which, 1, part] = m_low
+            mats[which, part] = jnp.concatenate([m_high, m_high, m_low], axis=0)
     w0_t = wl_t[:, 0:ch]
-    w0 = nt_dot(eye, w0_t, HIGHEST)
-    ec = nt_dot(eye, ec_ref[...], HIGHEST)
+    w0 = turn(eye16, w0_t)
+    ec = turn(eye16, ec_ref[...])
     w0pad[...] = jnp.zeros((2, ch, LANES), F32)
-    w0pad[0, :, GROUP : GROUP + ch] = w0_t
-    w0pad[1, :, GROUP + ch : GROUP + 2 * ch] = w0
+    w0pad[0, :, 80 : 80 + ch] = w0_t
+    w0pad[1, :, 80 : 80 + ch] = w0
     w1f = jnp.concatenate(
         [
-            nt_dot(eye, wb_ref[...], HIGHEST),
-            nt_dot(eye, en_ref[...], HIGHEST),
+            nt_dot(eye16, wb_ref[...].astype(BF16)),
+            nt_dot(eye16, en_ref[...].astype(BF16)),
             jnp.zeros((ch, 16 - n_basis - n_kinds), F32),
         ],
         axis=1,
     )
-    w1s[...] = left_parts(w1f)
+    w1s[...] = w1f.astype(BF16)
     row32 = lax.broadcasted_iota(I32, (32, LANES), 0)
     lane32 = lax.broadcasted_iota(I32, (32, LANES), 1)
     g3[1, 0:32, :] = jnp.zeros((32, LANES), F32)
     g3[1, 0:n_basis, 0:ch] = wb_ref[...]
     head = g3[1, 0:32, :] + jnp.where(
         (row32 == 8) & (lane32 >= ch) & (lane32 < 2 * ch), 1.0, 0.0
-    ) + jnp.where((lane32 >= 2 * ch) & (row32 == 16 + ((lane32 - 2 * ch) >> 4)), 1.0, 0.0)
-    rest = jnp.where(row32 == 16 + ((lane32 + LANES - 2 * ch) >> 4), 1.0, 0.0)
-    w_last = jnp.concatenate([head, rest], axis=1).astype(BF16)[:, 0 : 2 * ch + LANES]
+    ) + jnp.where((lane32 >= 2 * ch) & (row32 == 16 + ((lane32 - 2 * ch) >> 3)), 1.0, 0.0)
+    w_last = head
     wcol[...] = jnp.broadcast_to(
         jnp.sum(jnp.where(eye > 0, wo_ref[...], 0.0), axis=1, keepdims=True), (ch, LANES)
     )
@@ -425,30 +425,29 @@
 
     n_harm = 8
     wide = n_harm * GROUP
-    own_lane = lax.broadcasted_iota(I32, (GROUP, LANES), 0) == (
-        lax.broadcasted_iota(I32, (GROUP, LANES), 1) & (GROUP - 1)
-    )
+    own_lane = (lane8 & (GROUP - 1)) == sub8
     every = jnp.concatenate([own_lane] * n_harm, axis=0)
-    ones_row = jnp.where(own_lane, 1.0, 0.0).astype(BF16)
-    at_ef = wide + GROUP
+    ones_row = jnp.concatenate([jnp.where(own_lane, 1.0, 0.0), jnp.zeros((8, LANES), F32)], axis=0).astype(BF16)
+    at_ef = wide + 2 * GROUP
     at_dlp = at_ef + ch
+
+    degree_rows = ((1, 0, 3 * GROUP), (2, 3 * GROUP, wide), (0, wide, wide + 2 * GROUP))
 
     def by_degree(which, sums):
         parts = []
-        for degree, (a, b) in ((1, (0, 3)), (2, (3, n_harm)), (0, (n_harm, n_harm + 1))):
-            rows = sums[a * GROUP : b * GROUP]
-            parts.append(exact_dot(rows, which, degree))
-        return jnp.concatenate(parts, axis=0)
+        for degree, a, b in degree_rows:
+            grown = exact_dot(jnp.concatenate([x[a:b] for x in sums], axis=0), which, degree)
+            parts.append([grown[t * (b - a) : (t + 1) * (b - a)] for t in range(blocks)])
+        return [jnp.concatenate([p[t] for p in parts], axis=0) for t in range(blocks)]
 
     def exact_dot(rows, which, degree):
-        high, low = halves(rows)
-        m_high, m_low = mats[which, 0, degree], mats[which, 1, degree]
-        return nn_dot(high, m_high) + nn_dot(low, m_high) + nn_dot(high, m_low)
+        high = rows.astype(BF16).astype(F32)
+        joined = jnp.concatenate([high, rows - high, high], axis=1).astype(BF16)
+        return nn_dot(joined, mats[which, degree])
 
     def as_left(turned, pad):
-        tall_one = jnp.concatenate([turned, jnp.zeros((2 * LANES - wide - GROUP, ch), F32)], axis=0)
-        left = tall_one.T
-        return jnp.concatenate([left[:, 0:LANES], left[:, LANES:] + pad], axis=1).astype(BF16)
+        tall_one = jnp.concatenate([turned, jnp.zeros((LANES - at_ef, ch), F32)], axis=0)
+        return (tall_one.T + pad)[:, 0:at_dlp]
 
     w_out = wcol[...]
     kept = {}
@@ -461,7 +460,7 @@
         feats = jnp.concatenate(
             [zf[(base + jb) * 16 : (base + jb + 1) * 16, :] for jb in range(per_block)], axis=1
         )
-        kept["pre", b] = nn_dot(w1s[...], right_parts(feats))
+        kept["pre", b] = nn_dot(w1s[...], feats.astype(BF16))
 
     def stage_feat(b):
         centre_term = cterm[b]
@@ -477,16 +476,23 @@
             s1_s[row] = s1
             ds_s[row] = (sig + s1 * (1.0 - sig)) * env
             rhs[b, at_ef : at_ef + ch, cols] = (s1 * env).astype(BF16)
-            for m in range(n_harm):
-                rhs[b, m * GROUP : (m + 1) * GROUP, cols] = jnp.where(own_lane, z[m : m + 1], 0.0).astype(BF16)
-            rhs[b, wide : wide + GROUP, cols] = ones_row
+            for m in range(0, n_harm, 2):
+                two = [jnp.where(own_lane, z[t : t + 1], 0.0) for t in (m, m + 1)]
+                rhs[b, m * GROUP : (m + 2) * GROUP, cols] = jnp.concatenate(two, axis=0).astype(BF16)
+            rhs[b, wide : wide + 2 * GROUP, cols] = ones_row
 
     def stage_env(b):
-        sums = nt_dot(rhs[b, 0:at_ef, :], rhs[b, at_ef : at_ef + ch, :])
-        grown = by_degree(0, sums)
-        kept["g", b] = grown[0:wide]
-        left = as_left(grown, w0pad[0])
-        kept["lp", b] = nn_dot(left[:, 0:at_dlp], rhs[b, 0:at_dlp, :])
+        kept["f", b] = nt_dot(rhs[b, 0:at_ef, :], rhs[b, at_ef : at_ef + ch, :])
+
+    def stage_grow(b):
+        if b == 0:
+            grown = by_degree(0, [kept.pop(("f", t)) for t in range(blocks)])
+            for t in range(blocks):
+                kept["g", t] = grown[t]
+
+    def stage_lp(b):
+        left = as_left(kept["g", b], w0pad[0])
+        kept["lp", b] = split_dot(left, rhs[b, 0:at_dlp, :])
 
     def stage_latent(b):
         lp_all = kept.pop(("lp", b))
@@ -502,12 +508,20 @@
             rhs[b, at_dlp : at_dlp + ch, cols] = dlp.astype(BF16)
 
     def stage_back(b):
-        sums = nt_dot(rhs[b, 0:at_ef, :], rhs[b, at_dlp : at_dlp + ch, :])
-        grown = by_degree(1, sums)
+        kept["f", b] = nt_dot(rhs[b, 0:at_ef, :], rhs[b, at_dlp : at_dlp + ch, :])
+
+    def stage_shrink(b):
+        if b == 0:
+            grown = by_degree(1, [kept.pop(("f", t)) for t in range(blocks)])
+            for t in range(blocks):
+                kept["d", t] = grown[t]
+
+    def stage_de(b):
+        grown = kept.pop(("d", b))
         left = as_left(grown, w0pad[1])
-        kept["de", b] = nn_dot(left[:, 0 : at_dlp + ch], rhs[b])
-        both = jnp.concatenate([grown[0:wide], kept.pop(("g", b))], axis=1).astype(BF16)
-        kept["dy", b] = nn_dot(both, rhs[b, at_ef : at_dlp + ch, :])
+        kept["de", b] = split_dot(left, jnp.concatenate([rhs[b, 0:at_ef, :], rhs[b, at_dlp : at_dlp + ch, :]], axis=0))
+        both = jnp.concatenate([grown[0:wide], kept.pop(("g", b))[0:wide]], axis=1)
+        kept["dy", b] = nn_dot(both.astype(BF16), rhs[b, at_ef : at_dlp + ch, :])
 
     def stage_edge(b):
         de_all = kept.pop(("de", b))
@@ -521,16 +535,27 @@
             dpt_s[b, 2 * ch :, cols] = jnp.where(every, dy_all[:, cols], 0.0).astype(BF16)
 
     def stage_fold(b):
-        got = nn_dot(w_last, dpt_s[b])
+        got = split_dot(w_last, dpt_s[b])
         for jb in range(per_block):
             row = b * per_block + jb
             zd[row * 24 : row * 24 + 24, :] = got[0:24, jb * LANES : (jb + 1) * LANES]
 
-    stages = (stage_pre, stage_feat, stage_env, stage_latent, stage_back, stage_edge, stage_fold)
-    for tick in range(len(stages) + blocks - 1):
+    stages = (
+        stage_pre,
+        stage_feat,
+        stage_env,
+        stage_grow,
+        stage_lp,
+        stage_latent,
+        stage_back,
+        stage_shrink,
+        stage_de,
+        stage_edge,
+        stage_fold,
+    )
+    for stage in stages:
         for b in range(blocks):
-            if 0 <= tick - b < len(stages):
-                stages[tick - b](b)
+            stage(b)
     for row in range(n_rows, chunks * 8):
         zd[row * 24 : row * 24 + 24, :] = jnp.zeros((24, LANES), F32)
 
@@ -569,20 +594,27 @@
     for i in range(chunks):
         backward_chunk(i, 0)
 
-    extra = chunks * 8
-    pt[extra * 8 :, :] = jnp.zeros((8 * 8, LANES), F32)
-    for block in range(blocks):
-        at = (extra + block) * 8
-        sums = [
-            -jnp.sum(g3[c, block * per_block : (block + 1) * per_block, :], axis=0, keepdims=True)
-            for c in range(3)
-        ]
+    halfway = blocks // 2
+    pt[chunks * 64 :, :] = jnp.zeros((64, LANES), F32)
+    sums = []
+    for c in range(3):
+        rows = jnp.concatenate(
+            [
+                jnp.sum(g3[c, b * per_block : (b + 1) * per_block, :], axis=0, keepdims=True)
+                for b in range(blocks)
+            ],
+            axis=0,
+        )
+        rows = -(rows + pltpu.roll(rows, LANES // 2, 1))
+        sums.append(jnp.where(lane1 < LANES // 2, rows[0:halfway], rows[halfway:]))
+    for b in range(halfway):
+        at = (n_rows + b) * 8
 
         def store(which, value):
-            pt[at + which : at + which + 1, :] = value
+            pt[at + which : at + which + 1, :] = value[b : b + 1]
 
         put_parts(store, sums)
-        spread = (lane8 & (GROUP - 1)) + block * GROUP
+        spread = (lane8 & (GROUP - 1)) + jnp.where(lane8 < LANES // 2, b, b + halfway) * GROUP
         dest = pick(whole(0, 4), spread)[0:1].astype(I32)
         pt[at + 6 : at + 7, :] = (dest >> 7).astype(F32)
         pt[at + 7 : at + 8, :] = (dest & (LANES - 1)).astype(F32)
@@ -596,22 +628,19 @@
     zero16 = jnp.zeros((16, LANES), BF16)
     one16 = jnp.ones((16, LANES), BF16)
 
-    def scatter_body(i, acc):
+    spread_out = None
+    rows_left = n_rows + halfway + (n_rows + halfway) % 2
+    for first_row in range(0, rows_left, 8):
         lefts, rights = [], []
-        for t in range(8):
-            v = pt[pl.ds(pl.multiple_of((i * 8 + t) * 8, 8), 8), :]
+        for row in range(first_row, min(first_row + 8, rows_left)):
+            v = pt[row * 8 : row * 8 + 8, :]
             where_to = jnp.broadcast_to(v[6:7], (16, LANES)).astype(BF16)
             lo = jnp.broadcast_to(v[7:8], (16, LANES)).astype(BF16)
             twice = jnp.concatenate([v, v], axis=0).astype(BF16)
             lefts.append(jnp.concatenate([jnp.where(where_to == p, twice, zero16) for p in pairs], axis=0))
             rights.append(jnp.concatenate([jnp.where(lo == p, one16, zero16) for p in steps], axis=0))
-        left = jnp.concatenate(lefts, axis=1)
-        right = jnp.concatenate(rights, axis=1)
-        return acc + nt_dot(left, right)
-
-    spread_out = lax.fori_loop(
-        0, chunks + 1, scatter_body, jnp.zeros((len(pairs) * 16, tall), F32)
-    )
+        part = nt_dot(jnp.concatenate(lefts, axis=1), jnp.concatenate(rights, axis=1))
+        spread_out = part if spread_out is None else spread_out + part
     for t in range(n_targets):
         ret_out[t] = jnp.zeros((8, LANES), F32)
         ret_out[t, :, 0:tall] = spread_out[t * 8 : t * 8 + 8, :]
@@ -644,15 +673,15 @@
     force = force[0:3] + force[3:6]
     fresh = held[0:3] + 0.5 * TIME_STEP * force * held[6:7]
     for c in range(3):
-        nv_ref[0, c] = fresh[c : c + 1, 0:atoms]
-        ntr_ref[0, c] = held[c + 3 : c + 4, 0:atoms]
+        both_ref[0, c] = fresh[c : c + 1, 0:atoms]
+        both_ref[0, c + 3] = held[c + 3 : c + 4, 0:atoms]
 
 
 def on_device(*args):
     atoms = args[0].shape[3]
     slots = args[4].shape[2]
     ch = args[13].shape[0]
-    chunks = (atoms // GROUP * (slots // 8) + 7) // 8
+    chunks = (atoms // GROUP * (slots // 16) + 7) // 8
     n_gx, n_yz = lax.axis_size("gx"), lax.axis_size("yz")
     period = (n_gx * PX * SPACING, n_yz * PY * SPACING, PZ * SPACING)
     pos, vel, frc, spc, nbr, msk, sx, sy, ms, mr, wb, ec, en, we, wl, wo = args
@@ -664,18 +693,18 @@
         kernel_body(period, atoms, slots, *refs)
 
     vmem = pl.BlockSpec(memory_space=pltpu.VMEM)
-    per_block = slots // 8
+    per_block = slots // 16
     blocks = atoms // GROUP
     dma = pltpu.SemaphoreType.DMA
-    out = jax.ShapeDtypeStruct((1, 3, 1, atoms), F32)
+    out = jax.ShapeDtypeStruct((1, 6, 1, atoms), F32)
     staged = tuple(
         (pltpu.SMEM if at in (8, 9) else pltpu.VMEM)(x.shape, x.dtype) for at, x in enumerate(args)
     )
-    velocity, travel = pl.pallas_call(
+    both = pl.pallas_call(
         body,
-        out_shape=(out, out),
+        out_shape=out,
         in_specs=[pl.BlockSpec(memory_space=pl.ANY)] * 16,
-        out_specs=(vmem, vmem),
+        out_specs=vmem,
         scratch_shapes=[
             staged,
             pltpu.VMEM((9, 8, LANES), F32),
@@ -691,11 +720,11 @@
             pltpu.VMEM((chunks * 192, LANES), F32),
             pltpu.VMEM((chunks * 64 + 64, LANES), F32),
             pltpu.VMEM((atoms // GROUP, ch, LANES), F32),
-            pltpu.VMEM((2, 2, 3, ch, ch), BF16),
-            pltpu.VMEM((ch, 48), BF16),
+            pltpu.VMEM((2, 3, 3 * ch, ch), BF16),
+            pltpu.VMEM((ch, 16), BF16),
             pltpu.VMEM((ch, LANES), F32),
             pltpu.VMEM((2, ch, LANES), F32),
-            pltpu.VMEM((blocks, 9 * GROUP + 2 * ch, per_block * LANES), BF16),
+            pltpu.VMEM((blocks, 10 * GROUP + 2 * ch, per_block * LANES), BF16),
             pltpu.VMEM((blocks * per_block, ch, LANES), F32),
             pltpu.VMEM((blocks * per_block, ch, LANES), F32),
             pltpu.VMEM((blocks * per_block, ch, LANES), F32),
@@ -713,7 +742,7 @@
             collective_id=0, has_side_effects=True, vmem_limit_bytes=60 * 1024 * 1024
         ),
     )(*args)
-    return velocity.transpose(0, 2, 1, 3), travel.transpose(0, 2, 1, 3)
+    return both[:, 0:3].transpose(0, 2, 1, 3), both[:, 3:6].transpose(0, 2, 1, 3)
 
 
 def solution(mesh):

time: 34.4 us -> 28.4 us (0.83)
  Pallas kernels: 31.7 us -> 26.3 us
  local copies, waits for them, and re-layouts: 1.85 us -> 1.25 us
    pallas_call x1, Pallas kernels: 31.7 us -> 26.3 us  [on_device(): pl.pallas_call(body, out_shape=out, in_specs=[pl.BlockSpec(memory_space=p...]
    unnamed x6 -> x1, local copies, waits for them, and re-layouts: 1.85 us -> 1.25 us
where the time goes in v2:
time: 28.4 us; the launch traced here: 28.2 us
  Pallas kernels  26.3 us (93%)
  local copies, waits for them, and re-layouts  1.25 us (4%)
  between operations  0.64 us (2%)
    pallas_call x1, Pallas kernels, on_device(): pl.pallas_call(body, out_shape=out, in_specs=[pl.BlockSpec(memory_space=p...  26.3 us
    unnamed x1, local copies, waits for them, and re-layouts  1.25 us

profile of v2, /device:TPU:8, one launch (start us, length us, event | category | flops | bytes accessed | tf_op | source)
XLA Modules:
  0.0 28.2 jit_solution(7493151866524289711)
XLA Ops:
  0.6 26.3 %shard_map.167 = f32[1,6,1,80]{3,2,1,0:T(1,128)} custom-call(f32[1,3,1,80]{3,2,1,0:T(1,128)} %bitcast.22, f32[1,3,1,80]{3,2,1,0:T(1,128)} %bitcast.23, f32[1,3,1,80]{3,2,1,0:T(1,128)} %bitcast.24, s32[1,1,80]{2,1,0:T(1,128)} %refs_3_.1, s32[1,1,80,96]{3,2,1,0:T(8,128)} %bitcast.17, s32[1,1,80,96]{3,2,1,0:T(8,128)} %bitcast.18, s32[1,1,2,40]{3,2,1,0:T(2,128)} %refs_6_.1, ...), custom_call_target="tpu_custom_call" | custom-call | tf_op jit(solution)/shard_map/pallas_call | solution.py:703
  27.0 1.2 %slice_bitcast_fusion = (f32[1,1,3,80]{3,1,2,0:T(1,128)}, f32[1,1,3,80]{3,1,2,0:T(1,128)}) fusion(f32[1,6,1,80]{3,2,1,0:T(1,128)} %shard_map.167), kind=kLoop, calls=%fused_computation | loop fusion | bytes 3840

commit v3 on v2

--- a/solution.py
+++ b/solution.py
@@ -28,9 +28,9 @@
 R15 = 15.0**0.5
 
 HALO = [(dx, dy) for dy in (-1, 0, 1) for dx in (-1, 0, 1)]
-NEAR = [pos for pos in HALO if pos != (0, 0)]
+NEAR = sorted((pos for pos in HALO if pos != (0, 0)), key=lambda pos: -abs(pos[0]) - 2 * abs(pos[1]))
 TARGETS = [(dx, dy) for dy in (-1, 0, 1) for dx in (-2, -1, 0, 1, 2)]
-FAR = [pos for pos in TARGETS if pos != (0, 0)]
+FAR = sorted((pos for pos in TARGETS if pos != (0, 0)), key=lambda pos: -(abs(pos[0]) % 2) - 2 * abs(pos[1]))
 
 
 def halo_slot(dx, dy):
@@ -133,11 +133,11 @@
     first = (0, 1, 2, 3, 6, 7, 8, 9)
     for at, (far, close) in enumerate(zip(raw, staged)):
         loads.append(pltpu.make_async_copy(far, close, load_sems.at[at]))
+    for dx, dy in FAR:
+        pl.semaphore_signal(barrier, inc=1, device_id=device(dx, dy), device_id_type=MESH)
+
     for at in first:
         loads[at].start()
-    for dx, dy in FAR:
-        pl.semaphore_signal(barrier, inc=1, device_id=device(dx, dy), device_id_type=MESH)
-
     for at in range(16):
         if at not in first:
             loads[at].start()
@@ -210,7 +210,7 @@
     load[1] = pick(load[1], jnp.broadcast_to(place, (8, LANES)))
 
     pl.semaphore_wait(barrier, len(FAR))
-    sends = []
+    sends, carried = [], []
     for dx, dy in NEAR:
         there = halo_slot(-dx, -dy)
         copy = pltpu.make_async_remote_copy(
@@ -234,7 +234,7 @@
             device_id_type=MESH,
         )
         copy.start()
-        sends.append(copy)
+        carried.append(copy)
 
     for at in range(16):
         if at not in first:
@@ -298,8 +298,21 @@
         jnp.sum(jnp.where(eye > 0, wo_ref[...], 0.0), axis=1, keepdims=True), (ch, LANES)
     )
 
+    kind_rows = jnp.broadcast_to(halo[own, 3:4, :], (8, LANES))
+    for block in range(blocks):
+        spread = (lane8 & (GROUP - 1)) + block * GROUP
+        kind_row = jnp.broadcast_to(pick(kind_rows, spread)[0:1], (ch, LANES))
+        term = jnp.zeros((ch, LANES), F32)
+        for kind in range(n_kinds):
+            term = jnp.where(
+                kind_row == float(kind),
+                jnp.broadcast_to(ec[:, kind : kind + 1], (ch, LANES)),
+                term,
+            )
+        cterm[block] = term
+
     for copy in sends:
-        copy.wait()
+        copy.wait_recv()
 
     def shifted(dx, dy):
         step = float(LANES * ((dy + 1) * 5 + dx + 1))
@@ -411,22 +424,10 @@
     for i in range(chunks):
         forward_chunk(i, 0)
 
-    for block in range(blocks):
-        spread = (lane8 & (GROUP - 1)) + block * GROUP
-        kind_row = jnp.broadcast_to(pick(whole(0, 3), spread)[0:1], (ch, LANES))
-        term = jnp.zeros((ch, LANES), F32)
-        for kind in range(n_kinds):
-            term = jnp.where(
-                kind_row == float(kind),
-                jnp.broadcast_to(ec[:, kind : kind + 1], (ch, LANES)),
-                term,
-            )
-        cterm[block] = term
-
     n_harm = 8
     wide = n_harm * GROUP
     own_lane = (lane8 & (GROUP - 1)) == sub8
-    every = jnp.concatenate([own_lane] * n_harm, axis=0)
+    every = jnp.concatenate([jnp.where(own_lane, 1.0, 0.0)] * n_harm, axis=0).astype(BF16)
     ones_row = jnp.concatenate([jnp.where(own_lane, 1.0, 0.0), jnp.zeros((8, LANES), F32)], axis=0).astype(BF16)
     at_ef = wide + 2 * GROUP
     at_dlp = at_ef + ch
@@ -437,8 +438,8 @@
         parts = []
         for degree, a, b in degree_rows:
             grown = exact_dot(jnp.concatenate([x[a:b] for x in sums], axis=0), which, degree)
-            parts.append([grown[t * (b - a) : (t + 1) * (b - a)] for t in range(blocks)])
-        return [jnp.concatenate([p[t] for p in parts], axis=0) for t in range(blocks)]
+            parts.append([grown[t * (b - a) : (t + 1) * (b - a)] for t in range(len(sums))])
+        return [jnp.concatenate([p[t] for p in parts], axis=0) for t in range(len(sums))]
 
     def exact_dot(rows, which, degree):
         high = rows.astype(BF16).astype(F32)
@@ -485,10 +486,11 @@
         kept["f", b] = nt_dot(rhs[b, 0:at_ef, :], rhs[b, at_ef : at_ef + ch, :])
 
     def stage_grow(b):
-        if b == 0:
-            grown = by_degree(0, [kept.pop(("f", t)) for t in range(blocks)])
-            for t in range(blocks):
-                kept["g", t] = grown[t]
+        half = blocks // 2
+        if b % half == 0:
+            grown = by_degree(0, [kept.pop(("f", t)) for t in range(b, b + half)])
+            for t in range(half):
+                kept["g", b + t] = grown[t]
 
     def stage_lp(b):
         left = as_left(kept["g", b], w0pad[0])
@@ -511,10 +513,11 @@
         kept["f", b] = nt_dot(rhs[b, 0:at_ef, :], rhs[b, at_dlp : at_dlp + ch, :])
 
     def stage_shrink(b):
-        if b == 0:
-            grown = by_degree(1, [kept.pop(("f", t)) for t in range(blocks)])
-            for t in range(blocks):
-                kept["d", t] = grown[t]
+        half = blocks // 2
+        if b % half == 0:
+            grown = by_degree(1, [kept.pop(("f", t)) for t in range(b, b + half)])
+            for t in range(half):
+                kept["d", b + t] = grown[t]
 
     def stage_de(b):
         grown = kept.pop(("d", b))
@@ -532,7 +535,7 @@
             de = de_all[:, cols] + w_out * env_row(row)
             dpt_s[b, 0:ch, cols] = (de * ds_s[row]).astype(BF16)
             dpt_s[b, ch : 2 * ch, cols] = (hid_s[row] + de * s1_s[row]).astype(BF16)
-            dpt_s[b, 2 * ch :, cols] = jnp.where(every, dy_all[:, cols], 0.0).astype(BF16)
+            dpt_s[b, 2 * ch :, cols] = dy_all[:, cols].astype(BF16) * every
 
     def stage_fold(b):
         got = split_dot(w_last, dpt_s[b])
@@ -553,9 +556,12 @@
         stage_edge,
         stage_fold,
     )
-    for stage in stages:
-        for b in range(blocks):
-            stage(b)
+    teams = (range(0, blocks // 2), range(blocks // 2, blocks))
+    for tick in range(len(stages) + 3):
+        for late, team in enumerate(teams):
+            if 0 <= tick - 3 * late < len(stages):
+                for b in team:
+                    stages[tick - 3 * late](b)
     for row in range(n_rows, chunks * 8):
         zd[row * 24 : row * 24 + 24, :] = jnp.zeros((24, LANES), F32)
 
@@ -645,7 +651,7 @@
         ret_out[t] = jnp.zeros((8, LANES), F32)
         ret_out[t, :, 0:tall] = spread_out[t * 8 : t * 8 + 8, :]
 
-    sends = []
+    returns = []
     for dx, dy in FAR:
         there = target_slot(-dx, -dy)
         copy = pltpu.make_async_remote_copy(
@@ -657,16 +663,18 @@
             device_id_type=MESH,
         )
         copy.start()
-        sends.append(copy)
-
+        returns.append(copy)
+
+    for copy in carried:
+        copy.wait_recv()
     settle = jnp.broadcast_to(source, (8, LANES))
     mine, low, high = load[1], load[0], load[2]
     held = jnp.where(lane8 < atoms, mine, jnp.where(lane8 < atoms + 5, low, high))
     held = jnp.where(lane8 < LANES - 1, held, 0.0)
     held = pick(held, settle)
     total = ret_out[target_slot(0, 0)]
-    for copy, (dx, dy) in zip(sends, FAR):
-        copy.wait()
+    for copy in returns:
+        copy.wait_recv()
     for dx, dy in FAR:
         total = total + ret_in[target_slot(dx, dy)]
     force = pick(total, settle)
@@ -675,6 +683,8 @@
     for c in range(3):
         both_ref[0, c] = fresh[c : c + 1, 0:atoms]
         both_ref[0, c + 3] = held[c + 3 : c + 4, 0:atoms]
+    for copy in sends + carried + returns:
+        copy.wait_send()
 
 
 def on_device(*args):

time: 28.4 us -> 28 us (0.986)
  Pallas kernels: 26.3 us -> 25.9 us
    pallas_call x1, Pallas kernels: 26.3 us -> 25.9 us  [on_device(): pl.pallas_call(body, out_shape=out, in_specs=[pl.BlockSpec(memory_space=p...]
where the time goes in v3:
time: 28 us; the launch traced here: 27.8 us
  Pallas kernels  25.9 us (92%)
  local copies, waits for them, and re-layouts  1.25 us (4%)
  between operations  0.64 us (2%)
    pallas_call x1, Pallas kernels, on_device(): pl.pallas_call(body, out_shape=out, in_specs=[pl.BlockSpec(memory_space=p...  25.9 us
    unnamed x1, local copies, waits for them, and re-layouts  1.25 us

profile of v3, /device:TPU:8, one launch (start us, length us, event | category | flops | bytes accessed | tf_op | source)
XLA Modules:
  0.0 27.8 jit_solution(2857300232267629299)
XLA Ops:
  0.6 25.9 %shard_map.167 = f32[1,6,1,80]{3,2,1,0:T(1,128)} custom-call(f32[1,3,1,80]{3,2,1,0:T(1,128)} %bitcast.22, f32[1,3,1,80]{3,2,1,0:T(1,128)} %bitcast.23, f32[1,3,1,80]{3,2,1,0:T(1,128)} %bitcast.24, s32[1,1,80]{2,1,0:T(1,128)} %refs_3_.1, s32[1,1,80,96]{3,2,1,0:T(8,128)} %bitcast.17, s32[1,1,80,96]{3,2,1,0:T(8,128)} %bitcast.18, s32[1,1,2,40]{3,2,1,0:T(2,128)} %refs_6_.1, ...), custom_call_target="tpu_custom_call" | custom-call | tf_op jit(solution)/shard_map/pallas_call | solution.py:713
  26.6 1.2 %slice_bitcast_fusion = (f32[1,1,3,80]{3,1,2,0:T(1,128)}, f32[1,1,3,80]{3,1,2,0:T(1,128)}) fusion(f32[1,6,1,80]{3,2,1,0:T(1,128)} %shard_map.167), kind=kLoop, calls=%fused_computation | loop fusion | bytes 3840

commit v4 on v3

--- a/solution.py
+++ b/solution.py
@@ -30,7 +30,17 @@
 HALO = [(dx, dy) for dy in (-1, 0, 1) for dx in (-1, 0, 1)]
 NEAR = sorted((pos for pos in HALO if pos != (0, 0)), key=lambda pos: -abs(pos[0]) - 2 * abs(pos[1]))
 TARGETS = [(dx, dy) for dy in (-1, 0, 1) for dx in (-2, -1, 0, 1, 2)]
-FAR = sorted((pos for pos in TARGETS if pos != (0, 0)), key=lambda pos: -(abs(pos[0]) % 2) - 2 * abs(pos[1]))
+REST = sorted((pos for pos in TARGETS if pos != (0, 0)), key=lambda pos: -(abs(pos[0]) % 2) - 2 * abs(pos[1]))
+
+
+FAR = [pos for pos in REST if abs(pos[0]) == 2]
+NIGH = [pos for pos in REST if abs(pos[0]) < 2]
+DROPPED = 127
+EMPTY = 95
+
+
+def far_slot(dx, dy):
+    return (dy + 1) * 2 + (dx + 2) // 4
 
 
 def halo_slot(dx, dy):
@@ -89,6 +99,8 @@
         load,
         ret_out,
         ret_in,
+        far_out,
+        far_in,
         nb_pad,
         rows_code,
         table,
@@ -115,6 +127,8 @@
         load_recv,
         ret_send,
         ret_recv,
+        far_send,
+        far_recv,
     ) = refs
     gx = lax.axis_index("gx")
     yz = lax.axis_index("yz")
@@ -133,7 +147,7 @@
     first = (0, 1, 2, 3, 6, 7, 8, 9)
     for at, (far, close) in enumerate(zip(raw, staged)):
         loads.append(pltpu.make_async_copy(far, close, load_sems.at[at]))
-    for dx, dy in FAR:
+    for dx, dy in REST:
         pl.semaphore_signal(barrier, inc=1, device_id=device(dx, dy), device_id_type=MESH)
 
     for at in first:
@@ -187,14 +201,14 @@
     for side in (0, 1):
         for k in range(ms_ref.shape[3]):
             seat = atoms + 5 * (1 - side) + k
-            code = jnp.where(lane1 == mr_ref[0, 0, side, k], LANES - 1, code)
+            code = jnp.where(lane1 == mr_ref[0, 0, side, k], DROPPED, code)
     for side in (0, 1):
         for k in range(ms_ref.shape[3]):
             seat = atoms + 5 * (1 - side) + k
             gone = ms_ref[0, 0, side, k]
             code = jnp.where(lane1 == gone, (2 * side - 1) * LANES + seat, code)
             place = jnp.where(lane1 == seat, gone, place)
-            source = jnp.where(lane1 == gone, LANES - 1, source)
+            source = jnp.where(lane1 == gone, EMPTY, source)
     for side in (0, 1):
         for k in range(ms_ref.shape[3]):
             source = jnp.where(lane1 == mr_ref[0, 0, side, k], atoms + 5 * side + k, source)
@@ -209,7 +223,7 @@
     halo[own, 5:6, :] = lists[1:2] + pltpu.roll(lists, width_x, 1)[0:1]
     load[1] = pick(load[1], jnp.broadcast_to(place, (8, LANES)))
 
-    pl.semaphore_wait(barrier, len(FAR))
+    pl.semaphore_wait(barrier, len(REST))
     sends, carried = [], []
     for dx, dy in NEAR:
         there = halo_slot(-dx, -dy)
@@ -235,6 +249,9 @@
         )
         copy.start()
         carried.append(copy)
+
+    for t in range(len(TARGETS)):
+        ret_out[t] = jnp.zeros((4, LANES), F32)
 
     for at in range(16):
         if at not in first:
@@ -648,22 +665,33 @@
         part = nt_dot(jnp.concatenate(lefts, axis=1), jnp.concatenate(rights, axis=1))
         spread_out = part if spread_out is None else spread_out + part
     for t in range(n_targets):
-        ret_out[t] = jnp.zeros((8, LANES), F32)
-        ret_out[t, :, 0:tall] = spread_out[t * 8 : t * 8 + 8, :]
+        tile = spread_out[t * 8 : t * 8 + 8, :]
+        ret_out[t, 0:3, 0:tall] = tile[0:3] + tile[3:6]
+    for dx, dy in FAR:
+        tile = jnp.concatenate([ret_out[target_slot(dx, dy)], jnp.zeros((4, LANES), F32)], axis=0)
+        far_out[far_slot(dx, dy)] = jnp.where(
+            lane1 < atoms + 10,
+            tile[0:1],
+            jnp.where(lane1 < atoms + 20, pltpu.roll(tile, 10, 1)[1:2], pltpu.roll(tile, 20, 1)[2:3]),
+        )
 
     returns = []
-    for dx, dy in FAR:
-        there = target_slot(-dx, -dy)
-        copy = pltpu.make_async_remote_copy(
-            src_ref=ret_out.at[target_slot(dx, dy)],
-            dst_ref=ret_in.at[there],
-            send_sem=ret_send.at[there],
-            recv_sem=ret_recv.at[there],
-            device_id=device(dx, dy),
-            device_id_type=MESH,
-        )
-        copy.start()
-        returns.append(copy)
+    for group, slot, out, into, send_sems, recv_sems in (
+        (NIGH, target_slot, ret_out, ret_in, ret_send, ret_recv),
+        (FAR, far_slot, far_out, far_in, far_send, far_recv),
+    ):
+        for dx, dy in group:
+            there = slot(-dx, -dy)
+            copy = pltpu.make_async_remote_copy(
+                src_ref=out.at[slot(dx, dy)],
+                dst_ref=into.at[there],
+                send_sem=send_sems.at[there],
+                recv_sem=recv_sems.at[there],
+                device_id=device(dx, dy),
+                device_id_type=MESH,
+            )
+            copy.start()
+            returns.append(copy)
 
     for copy in carried:
         copy.wait_recv()
@@ -675,10 +703,16 @@
     total = ret_out[target_slot(0, 0)]
     for copy in returns:
         copy.wait_recv()
-    for dx, dy in FAR:
+    for dx, dy in NIGH:
         total = total + ret_in[target_slot(dx, dy)]
-    force = pick(total, settle)
-    force = force[0:3] + force[3:6]
+    far = far_in[0]
+    for t in range(1, len(FAR)):
+        far = far + far_in[t]
+    far = jnp.broadcast_to(far, (8, LANES))
+    seats = jnp.logical_and(lane8 >= atoms, lane8 < atoms + 10)
+    moved = jnp.where(sub8 == 0, far, jnp.where(sub8 == 1, pltpu.roll(far, LANES - 10, 1), pltpu.roll(far, LANES - 20, 1)))
+    total = jnp.concatenate([total, jnp.zeros((4, LANES), F32)], axis=0) + jnp.where(seats, moved, 0.0)
+    force = pick(total, settle)[0:3]
     fresh = held[0:3] + 0.5 * TIME_STEP * force * held[6:7]
     for c in range(3):
         both_ref[0, c] = fresh[c : c + 1, 0:atoms]
@@ -719,8 +753,10 @@
             staged,
             pltpu.VMEM((9, 8, LANES), F32),
             pltpu.VMEM((3, 8, LANES), F32),
-            pltpu.VMEM((15, 8, LANES), F32),
-            pltpu.VMEM((15, 8, LANES), F32),
+            pltpu.VMEM((15, 4, LANES), F32),
+            pltpu.VMEM((15, 4, LANES), F32),
+            pltpu.VMEM((6, 1, LANES), F32),
+            pltpu.VMEM((6, 1, LANES), F32),
             pltpu.VMEM((atoms, LANES), F32),
             pltpu.VMEM((chunks * 8, LANES), F32),
             pltpu.VMEM((4, 8, LANES), F32),
@@ -747,6 +783,8 @@
             dma((3,)),
             dma((15,)),
             dma((15,)),
+            dma((6,)),
+            dma((6,)),
         ],
         compiler_params=pltpu.CompilerParams(
             collective_id=0, has_side_effects=True, vmem_limit_bytes=60 * 1024 * 1024

time: 28 us -> 28.1 us (level)
  no operation moved by 1% of the time
where the time goes in v4:
time: 28.1 us; the launch traced here: 27.9 us
  Pallas kernels  26 us (93%)
  local copies, waits for them, and re-layouts  1.25 us (4%)
  between operations  0.64 us (2%)
    pallas_call x1, Pallas kernels, on_device(): pl.pallas_call(body, out_shape=out, in_specs=[pl.BlockSpec(memory_space=p...  26 us
    unnamed x1, local copies, waits for them, and re-layouts  1.25 us

profile of v4, /device:TPU:8, one launch (start us, length us, event | category | flops | bytes accessed | tf_op | source)
XLA Modules:
  0.0 27.9 jit_solution(16017299417089180245)
XLA Ops:
  0.6 26.0 %shard_map.167 = f32[1,6,1,80]{3,2,1,0:T(1,128)} custom-call(f32[1,3,1,80]{3,2,1,0:T(1,128)} %bitcast.22, f32[1,3,1,80]{3,2,1,0:T(1,128)} %bitcast.23, f32[1,3,1,80]{3,2,1,0:T(1,128)} %bitcast.24, s32[1,1,80]{2,1,0:T(1,128)} %refs_3_.1, s32[1,1,80,96]{3,2,1,0:T(8,128)} %bitcast.17, s32[1,1,80,96]{3,2,1,0:T(8,128)} %bitcast.18, s32[1,1,2,40]{3,2,1,0:T(2,128)} %refs_6_.1, ...), custom_call_target="tpu_custom_call" | custom-call | tf_op jit(solution)/shard_map/pallas_call | solution.py:747
  26.7 1.2 %slice_bitcast_fusion = (f32[1,1,3,80]{3,1,2,0:T(1,128)}, f32[1,1,3,80]{3,1,2,0:T(1,128)}) fusion(f32[1,6,1,80]{3,2,1,0:T(1,128)} %shard_map.167), kind=kLoop, calls=%fused_computation | loop fusion | bytes 3840

commit v5 on v4

--- a/solution.py
+++ b/solution.py
@@ -96,6 +96,7 @@
         both_ref,
         staged,
         halo,
+        edge,
         load,
         ret_out,
         ret_in,
@@ -120,6 +121,8 @@
         hid_s,
         dpt_s,
         g3,
+        spot,
+        early,
         load_sems,
         halo_send,
         halo_recv,
@@ -220,7 +223,8 @@
     g3[0] = jnp.zeros((64, LANES), F32)
     g3[0, 0:2, 0:width_x] = sx_ref[0, 0].astype(F32)
     lists = g3[0, 0:8, :]
-    halo[own, 5:6, :] = lists[1:2] + pltpu.roll(lists, width_x, 1)[0:1]
+    outward = lists[1:2] + pltpu.roll(lists, width_x, 1)[0:1]
+    edge[...] = pick(halo[own], jnp.broadcast_to(outward, (8, LANES)).astype(I32))
     load[1] = pick(load[1], jnp.broadcast_to(place, (8, LANES)))
 
     pl.semaphore_wait(barrier, len(REST))
@@ -228,7 +232,7 @@
     for dx, dy in NEAR:
         there = halo_slot(-dx, -dy)
         copy = pltpu.make_async_remote_copy(
-            src_ref=halo.at[own],
+            src_ref=edge if dx else halo.at[own],
             dst_ref=halo.at[there],
             send_sem=halo_send.at[there],
             recv_sem=halo_recv.at[there],
@@ -315,6 +319,31 @@
         jnp.sum(jnp.where(eye > 0, wo_ref[...], 0.0), axis=1, keepdims=True), (ch, LANES)
     )
 
+    def shifted(dx, dy):
+        step = float(LANES * ((dy + 1) * 5 + dx + 1))
+        return halo[halo_slot(dx, dy)] + jnp.where(sub8 == 4, step, 0.0)
+
+    def whole(k, c):
+        return jnp.broadcast_to(table[k, c : c + 1, :], (8, LANES))
+
+    table[0] = shifted(0, 0)
+    for i in range(chunks):
+        word = rows_code[i * 8 : i * 8 + 8, :]
+        n = jnp.where(word >= 512.0, word - 512.0, word).astype(I32)
+        k = jnp.where(n >= atoms, 1, 0) + jnp.where(n >= 2 * atoms, 1, 0) + jnp.where(n >= 3 * atoms, 1, 0)
+        n = n - atoms * k
+        spot[0, i] = n
+        spot[1, i] = k
+        for c in range(5):
+            early[c, i] = pick(whole(0, c), n)
+        row = i * 8 + sub8
+        block = jnp.zeros((8, LANES), I32)
+        for b in range(1, blocks):
+            block = block + jnp.where(row >= b * per_block, 1, 0)
+        centre = block * GROUP + (lane8 & (GROUP - 1))
+        for c in range(3):
+            early[5 + c, i] = pick(whole(0, c), centre)
+
     kind_rows = jnp.broadcast_to(halo[own, 3:4, :], (8, LANES))
     for block in range(blocks):
         spread = (lane8 & (GROUP - 1)) + block * GROUP
@@ -331,20 +360,11 @@
     for copy in sends:
         copy.wait_recv()
 
-    def shifted(dx, dy):
-        step = float(LANES * ((dy + 1) * 5 + dx + 1))
-        return halo[halo_slot(dx, dy)] + jnp.where(sub8 == 4, step, 0.0)
-
     def row_index(rows, which):
         return jnp.broadcast_to(rows[which : which + 1, :], (8, LANES)).astype(I32)
 
     def x_ghosts(dy):
-        low, high = shifted(-1, dy), shifted(1, dy)
-        return jnp.where(
-            lane8 < width_x,
-            pick(low, row_index(low, 5)),
-            pick(high, row_index(high, 5)),
-        )
+        return jnp.where(lane8 < width_x, shifted(-1, dy), shifted(1, dy))
 
     def y_ghosts(dy):
         base = shifted(0, dy)
@@ -356,34 +376,23 @@
             pick(base, jnp.where(outer, 0, index)),
         )
 
-    table[0] = shifted(0, 0)
     table[1] = x_ghosts(0)
     table[2] = y_ghosts(-1)
     table[3] = y_ghosts(1)
 
-    def whole(k, c):
-        return jnp.broadcast_to(table[k, c : c + 1, :], (8, LANES))
-
     def forward_chunk(i, carry):
         word = rows_code[pl.ds(i * 8, 8), :]
         live = word >= 512.0
-        n = jnp.where(live, word - 512.0, word).astype(I32)
-        k = jnp.where(n >= atoms, 1, 0) + jnp.where(n >= 2 * atoms, 1, 0) + jnp.where(n >= 3 * atoms, 1, 0)
-        n = n - atoms * k
+        n, k = spot[0, i], spot[1, i]
         near = []
         for c in range(5):
-            v = pick(whole(0, c), n)
+            v = early[c, i]
             for part in (1, 2, 3):
                 v = jnp.where(k == part, pick(whole(part, c), n), v)
             near.append(v)
-        row = i * 8 + sub8
-        block = jnp.zeros((8, LANES), I32)
-        for b in range(1, blocks):
-            block = block + jnp.where(row >= b * per_block, 1, 0)
-        centre = block * GROUP + (lane8 & (GROUP - 1))
         off = []
         for c in range(3):
-            d = near[c] - pick(whole(0, c), centre)
+            d = near[c] - early[5 + c, i]
             d = d - period[c] * jnp.floor(d / period[c] + 0.5)
             off.append(jnp.where(live, d, SPACING if c == 0 else 0.0))
         radius = jnp.sqrt(off[0] * off[0] + off[1] * off[1] + off[2] * off[2])
@@ -752,6 +761,7 @@
         scratch_shapes=[
             staged,
             pltpu.VMEM((9, 8, LANES), F32),
+            pltpu.VMEM((8, LANES), F32),
             pltpu.VMEM((3, 8, LANES), F32),
             pltpu.VMEM((15, 4, LANES), F32),
             pltpu.VMEM((15, 4, LANES), F32),
@@ -776,6 +786,8 @@
             pltpu.VMEM((blocks * per_block, ch, LANES), F32),
             pltpu.VMEM((blocks, 2 * ch + 8 * GROUP, per_block * LANES), BF16),
             pltpu.VMEM((3, 64, LANES), F32),
+            pltpu.VMEM((2, chunks, 8, LANES), I32),
+            pltpu.VMEM((8, chunks, 8, LANES), F32),
             dma((16,)),
             dma((9,)),
             dma((9,)),

time: 28.1 us -> 28 us (level)
  no operation moved by 1% of the time
where the time goes in v5:
time: 28 us; the launch traced here: 27.8 us
  Pallas kernels  25.9 us (92%)
  local copies, waits for them, and re-layouts  1.25 us (4%)
  between operations  0.64 us (2%)
    pallas_call x1, Pallas kernels, on_device(): pl.pallas_call(body, out_shape=out, in_specs=[pl.BlockSpec(memory_space=p...  25.9 us
    unnamed x1, local copies, waits for them, and re-layouts  1.25 us

profile of v5, /device:TPU:8, one launch (start us, length us, event | category | flops | bytes accessed | tf_op | source)
XLA Modules:
  0.0 27.8 jit_solution(12730991694387313272)
XLA Ops:
  0.6 25.9 %shard_map.167 = f32[1,6,1,80]{3,2,1,0:T(1,128)} custom-call(f32[1,3,1,80]{3,2,1,0:T(1,128)} %bitcast.22, f32[1,3,1,80]{3,2,1,0:T(1,128)} %bitcast.23, f32[1,3,1,80]{3,2,1,0:T(1,128)} %bitcast.24, s32[1,1,80]{2,1,0:T(1,128)} %refs_3_.1, s32[1,1,80,96]{3,2,1,0:T(8,128)} %bitcast.17, s32[1,1,80,96]{3,2,1,0:T(8,128)} %bitcast.18, s32[1,1,2,40]{3,2,1,0:T(2,128)} %refs_6_.1, ...), custom_call_target="tpu_custom_call" | custom-call | tf_op jit(solution)/shard_map/pallas_call | solution.py:756
  26.6 1.2 %slice_bitcast_fusion = (f32[1,1,3,80]{3,1,2,0:T(1,128)}, f32[1,1,3,80]{3,1,2,0:T(1,128)}) fusion(f32[1,6,1,80]{3,2,1,0:T(1,128)} %shard_map.167), kind=kLoop, calls=%fused_computation | loop fusion | bytes 3840

commit v6 on v5

--- a/solution.py
+++ b/solution.py
@@ -150,7 +150,7 @@
     first = (0, 1, 2, 3, 6, 7, 8, 9)
     for at, (far, close) in enumerate(zip(raw, staged)):
         loads.append(pltpu.make_async_copy(far, close, load_sems.at[at]))
-    for dx, dy in REST:
+    for dx, dy in NEAR:
         pl.semaphore_signal(barrier, inc=1, device_id=device(dx, dy), device_id_type=MESH)
 
     for at in first:
@@ -227,7 +227,7 @@
     edge[...] = pick(halo[own], jnp.broadcast_to(outward, (8, LANES)).astype(I32))
     load[1] = pick(load[1], jnp.broadcast_to(place, (8, LANES)))
 
-    pl.semaphore_wait(barrier, len(REST))
+    pl.semaphore_wait(barrier, len(NEAR))
     sends, carried = [], []
     for dx, dy in NEAR:
         there = halo_slot(-dx, -dy)

time: 28 us -> 27.8 us (level)
  no operation moved by 1% of the time
where the time goes in v6:
time: 27.8 us; the launch traced here: 27.6 us
  Pallas kernels  25.7 us (92%)
  local copies, waits for them, and re-layouts  1.25 us (4%)
  between operations  0.64 us (2%)
    pallas_call x1, Pallas kernels, on_device(): pl.pallas_call(body, out_shape=out, in_specs=[pl.BlockSpec(memory_space=p...  25.7 us
    unnamed x1, local copies, waits for them, and re-layouts  1.25 us

profile of v6, /device:TPU:8, one launch (start us, length us, event | category | flops | bytes accessed | tf_op | source)
XLA Modules:
  0.0 27.6 jit_solution(6476999029047718248)
XLA Ops:
  0.6 25.7 %shard_map.167 = f32[1,6,1,80]{3,2,1,0:T(1,128)} custom-call(f32[1,3,1,80]{3,2,1,0:T(1,128)} %bitcast.22, f32[1,3,1,80]{3,2,1,0:T(1,128)} %bitcast.23, f32[1,3,1,80]{3,2,1,0:T(1,128)} %bitcast.24, s32[1,1,80]{2,1,0:T(1,128)} %refs_3_.1, s32[1,1,80,96]{3,2,1,0:T(8,128)} %bitcast.17, s32[1,1,80,96]{3,2,1,0:T(8,128)} %bitcast.18, s32[1,1,2,40]{3,2,1,0:T(2,128)} %refs_6_.1, ...), custom_call_target="tpu_custom_call" | custom-call | tf_op jit(solution)/shard_map/pallas_call | solution.py:756
  26.3 1.2 %slice_bitcast_fusion = (f32[1,1,3,80]{3,1,2,0:T(1,128)}, f32[1,1,3,80]{3,1,2,0:T(1,128)}) fusion(f32[1,6,1,80]{3,2,1,0:T(1,128)} %shard_map.167), kind=kLoop, calls=%fused_computation | loop fusion | bytes 3840

commit v7 on v6

--- a/solution.py
+++ b/solution.py
@@ -227,36 +227,6 @@
     edge[...] = pick(halo[own], jnp.broadcast_to(outward, (8, LANES)).astype(I32))
     load[1] = pick(load[1], jnp.broadcast_to(place, (8, LANES)))
 
-    pl.semaphore_wait(barrier, len(NEAR))
-    sends, carried = [], []
-    for dx, dy in NEAR:
-        there = halo_slot(-dx, -dy)
-        copy = pltpu.make_async_remote_copy(
-            src_ref=edge if dx else halo.at[own],
-            dst_ref=halo.at[there],
-            send_sem=halo_send.at[there],
-            recv_sem=halo_recv.at[there],
-            device_id=device(dx, dy),
-            device_id_type=MESH,
-        )
-        copy.start()
-        sends.append(copy)
-    for dx in (-1, 1):
-        there = 1 - dx
-        copy = pltpu.make_async_remote_copy(
-            src_ref=load.at[1],
-            dst_ref=load.at[there],
-            send_sem=load_send.at[there],
-            recv_sem=load_recv.at[there],
-            device_id=device(dx, 0),
-            device_id_type=MESH,
-        )
-        copy.start()
-        carried.append(copy)
-
-    for t in range(len(TARGETS)):
-        ret_out[t] = jnp.zeros((4, LANES), F32)
-
     for at in range(16):
         if at not in first:
             loads[at].wait()
@@ -356,6 +326,36 @@
                 term,
             )
         cterm[block] = term
+
+    pl.semaphore_wait(barrier, len(NEAR))
+    sends, carried = [], []
+    for dx, dy in NEAR:
+        there = halo_slot(-dx, -dy)
+        copy = pltpu.make_async_remote_copy(
+            src_ref=edge if dx else halo.at[own],
+            dst_ref=halo.at[there],
+            send_sem=halo_send.at[there],
+            recv_sem=halo_recv.at[there],
+            device_id=device(dx, dy),
+            device_id_type=MESH,
+        )
+        copy.start()
+        sends.append(copy)
+    for dx in (-1, 1):
+        there = 1 - dx
+        copy = pltpu.make_async_remote_copy(
+            src_ref=load.at[1],
+            dst_ref=load.at[there],
+            send_sem=load_send.at[there],
+            recv_sem=load_recv.at[there],
+            device_id=device(dx, 0),
+            device_id_type=MESH,
+        )
+        copy.start()
+        carried.append(copy)
+
+    for t in range(len(TARGETS)):
+        ret_out[t] = jnp.zeros((4, LANES), F32)
 
     for copy in sends:
         copy.wait_recv()

time: 27.8 us -> 27.8 us (level)
  no operation moved by 1% of the time
where the time goes in v7:
time: 27.8 us; the launch traced here: 27.6 us
  Pallas kernels  25.7 us (92%)
  local copies, waits for them, and re-layouts  1.25 us (4%)
  between operations  0.64 us (2%)
    pallas_call x1, Pallas kernels, on_device(): pl.pallas_call(body, out_shape=out, in_specs=[pl.BlockSpec(memory_space=p...  25.7 us
    unnamed x1, local copies, waits for them, and re-layouts  1.25 us

profile of v7, /device:TPU:8, one launch (start us, length us, event | category | flops | bytes accessed | tf_op | source)
XLA Modules:
  0.0 27.6 jit_solution(6606623513156816345)
XLA Ops:
  0.6 25.7 %shard_map.167 = f32[1,6,1,80]{3,2,1,0:T(1,128)} custom-call(f32[1,3,1,80]{3,2,1,0:T(1,128)} %bitcast.22, f32[1,3,1,80]{3,2,1,0:T(1,128)} %bitcast.23, f32[1,3,1,80]{3,2,1,0:T(1,128)} %bitcast.24, s32[1,1,80]{2,1,0:T(1,128)} %refs_3_.1, s32[1,1,80,96]{3,2,1,0:T(8,128)} %bitcast.17, s32[1,1,80,96]{3,2,1,0:T(8,128)} %bitcast.18, s32[1,1,2,40]{3,2,1,0:T(2,128)} %refs_6_.1, ...), custom_call_target="tpu_custom_call" | custom-call | tf_op jit(solution)/shard_map/pallas_call | solution.py:756
  26.3 1.2 %slice_bitcast_fusion = (f32[1,1,3,80]{3,1,2,0:T(1,128)}, f32[1,1,3,80]{3,1,2,0:T(1,128)}) fusion(f32[1,6,1,80]{3,2,1,0:T(1,128)} %shard_map.167), kind=kLoop, calls=%fused_computation | loop fusion | bytes 3840
